TPU v7x, 512 devices: a whole 4x8x8 slice. The times are simulated.
512 devices in a mesh: ctx: 32 (over x, y), tp: 16 (over z, core).
Axes of the slice: x: 4, y: 8, z: 8, core: 2. Of those that a mesh axis runs over, the one named last changes fastest.
Arguments:
- queries: bfloat16 [2, 512, 4096], P(None, 'ctx', 'tp'), may hold values from -20 to 20
- positions: int32 [2, 512], P(None, 'ctx'), may hold values from 0 to 32767, as said below
- cached_keys: bfloat16 [2, 32768, 4096], P(None, 'ctx', 'tp'), may hold values from -64 to 64
- cached_values: bfloat16 [2, 32768, 4096], P(None, 'ctx', 'tp'), may hold values from -24 to 24
- residual_rows: bfloat16 [2, 512, 4096], P(None, 'ctx', 'tp'), may hold values from -150 to 150
- out_proj: bfloat16 [4096, 4096], P('tp', 'ctx'), may hold values from -0.09375 to 0.09375
- norm_gain: bfloat16 [4096], P('tp'), may hold values from 0.5 to 1.5
- head_weight: bfloat16 [4096, 65536], P(None, ('ctx', 'tp')), may hold values from -1 to 1
- targets: int32 [2, 512], P(None, 'ctx'), may hold values from 0 to 65535
- live_rows: int32 [2], replicated, may hold values from 128 to 512, as said below
- mask_total: int32 [2], replicated, may hold values from 512 to 2048
Outputs:
- token_nll: float32 [2, 512], P(None, 'ctx')
- elbo_estimate: float32 [], replicated
Inputs may be any that keep to these rules, and one draw needn't show every extreme that they name: Within a sample the positions are distinct. One of the samples has all 512 slots live; slots below live_rows hold masked tokens.
All inputs are finite; a program needn't handle non-finite values.
Results may differ from a plain program's by a relative error of at most 0.001.
Values may be sent and summed in bfloat16 or wider, within the bound.
A program may use at most 64 MiB of HBM per device.

v0:
```python
import math

import jax
import jax.numpy as jnp
from jax import lax
from jax.sharding import PartitionSpec as P

HEAD_SIZE = 128


ROPE_BASE = 500000.0
NORM_EPSILON = 1e-05


def rotate(query_block, spot_table):
    halfway = query_block.shape[-1] // 2
    frequency = ROPE_BASE ** (-2.0 * jnp.arange(halfway, dtype=jnp.float32) / query_block.shape[-1])
    angles = spot_table.astype(jnp.float32)[..., None, None] * frequency
    cosine = jnp.cos(angles)
    sine_part = jnp.sin(angles)
    leading = query_block[..., :halfway]
    trailing = query_block[..., halfway:]
    return jnp.concatenate(
        [leading * cosine - trailing * sine_part, trailing * cosine + leading * sine_part], -1
    )


def on_device(
    queries,
    positions,
    cached_keys,
    cached_values,
    residual_rows,
    out_proj,
    norm_gain,
    head_weight,
    targets,
    live_rows,
    mask_total,
):
    samples, local_rows, local_width = queries.shape
    local_heads = local_width // HEAD_SIZE
    rotated = rotate(
        queries.astype(jnp.float32).reshape(samples, local_rows, local_heads, HEAD_SIZE), positions
    )
    rotated = rotated.astype(jnp.bfloat16).reshape(samples, local_rows, local_width)
    all_queries, all_targets = (
        lax.all_gather(rotated, "ctx", axis=1, tiled=True),
        lax.all_gather(targets, "ctx", axis=1, tiled=True),
    )
    all_rows = all_queries.shape[1]
    key_count = cached_keys.shape[1]
    query_heads = all_queries.reshape(samples, all_rows, local_heads, HEAD_SIZE)
    key_heads = cached_keys.reshape(samples, key_count, local_heads, HEAD_SIZE)
    value_heads = cached_values.reshape(samples, key_count, local_heads, HEAD_SIZE)
    attention_logits = jnp.einsum(
        "smhd,skhd->shmk", query_heads, key_heads, preferred_element_type=jnp.float32
    ) * (1.0 / math.sqrt(HEAD_SIZE))
    local_top = jnp.max(attention_logits, -1)
    row_top = lax.pmax(local_top, "ctx")
    weights = jnp.exp(attention_logits - row_top[..., None])
    totals = jnp.moveaxis(jnp.sum(weights, -1), 1, 2)
    softmax_numerator = jnp.einsum(
        "shmk,skhd->smhd",
        weights.astype(jnp.bfloat16),
        value_heads,
        preferred_element_type=jnp.float32,
    )
    softmax_numerator = softmax_numerator.reshape(samples, all_rows, local_width)
    numerator_rows, total_rows = (
        lax.psum_scatter(softmax_numerator, "ctx", scatter_dimension=1, tiled=True),
        lax.psum_scatter(totals, "ctx", scatter_dimension=1, tiled=True),
    )
    attended = (
        numerator_rows.reshape(samples, local_rows, local_heads, HEAD_SIZE) / total_rows[..., None]
    )
    attended = attended.astype(jnp.bfloat16).reshape(samples, local_rows, local_width)
    branch_part = jnp.einsum(
        "srd,dp->srp",
        attended,
        lax.all_gather(out_proj, "ctx", axis=1, tiled=True),
        preferred_element_type=jnp.float32,
    )
    vocab_width = head_weight.shape[1]
    branch = lax.psum(branch_part, "tp")
    full_resid, full_gain = (
        lax.all_gather(residual_rows, "tp", axis=2, tiled=True),
        lax.all_gather(norm_gain, "tp", axis=0, tiled=True),
    )
    stream = full_resid.astype(jnp.float32) + branch
    mean_square = jnp.mean(stream * stream, -1, keepdims=True)
    normed = (
        stream * lax.rsqrt(mean_square + NORM_EPSILON) * full_gain.astype(jnp.float32)
    ).astype(jnp.bfloat16)
    logits = jnp.einsum(
        "srd,dv->srv",
        lax.all_gather(normed, "ctx", axis=1, tiled=True),
        head_weight,
        preferred_element_type=jnp.float32,
    )
    vocab_start = lax.axis_index(("ctx", "tp")) * vocab_width
    column_ids = jnp.arange(vocab_width, dtype=jnp.int32)
    target_hit = column_ids == (all_targets - vocab_start)[..., None]
    picked = jnp.sum(jnp.where(target_hit, logits, 0.0), -1)
    local_peak = jnp.max(logits, -1)
    global_peak = lax.pmax(local_peak, ("ctx", "tp"))
    local_sum = jnp.sum(jnp.exp(logits - global_peak[..., None]), -1)
    exp_sum, target_logit = lax.psum((local_sum, picked), ("ctx", "tp"))
    alive_slots = jnp.arange(all_rows, dtype=jnp.int32)[None, :] < live_rows[:, None]
    nll_all = jnp.where(alive_slots, global_peak + jnp.log(exp_sum) - target_logit, 0.0)
    elbo_estimate = jnp.sum(jnp.sum(nll_all, 1) / mask_total.astype(jnp.float32)) / samples
    row_start = lax.axis_index("ctx") * local_rows
    token_nll = lax.dynamic_slice_in_dim(nll_all, row_start, local_rows, 1)
    return (token_nll, elbo_estimate)


def solution(mesh):
    in_specs = (
        P(None, "ctx", "tp"),
        P(None, "ctx"),
        P(None, "ctx", "tp"),
        P(None, "ctx", "tp"),
        P(None, "ctx", "tp"),
        P("tp", "ctx"),
        P("tp"),
        P(None, ("ctx", "tp")),
        P(None, "ctx"),
        P(),
        P(),
    )
    out_specs = (P(None, "ctx"), P())
    return jax.shard_map(
        on_device, mesh=mesh, in_specs=in_specs, out_specs=out_specs, check_vma=False
    )
```

profile of v0, /device:TPU:1, one launch (start us, length us, event | category | flops | bytes accessed | tf_op | source)
XLA Modules:
  0.0 1099.2 jit_solution(1527020038684243533)
XLA Ops:
  7.2 0.8 convert_element_type.29
  9.1 39.9 %all_gather.19 = bf16[2,512,256]{2,0,1:T(2,128)(2,1)S(1)} all-gather(bf16[2,16,256]{2,0,1:T(2,128)(2,1)S(1)} %copy.65), channel_id=1, replica_groups=mesh['ctx'=32,'tp'=16] {'ctx'}, dimensions={1}, use_global_device_ids=true | all-gather | bytes 540672 | tf_op jit(solution)/shard_map/all_gather | solution.py:48
  49.8 4.6 multiply_reduce_fusion
  54.4 59.6 %pmax.14 = f32[2,2,512]{2,1,0:T(2,128)S(1)} all-reduce(f32[2,2,512]{2,1,0:T(2,128)S(1)} %get-tuple-element.12), channel_id=1, replica_groups=mesh['ctx'=32,'tp'=16] {'ctx'}, use_global_device_ids=true, to_apply=%region_1.0 | all-reduce | flops 2048 | bytes 16384 | tf_op jit(solution)/shard_map/pmax | solution.py:60
  114.0 4.4 fusion
  118.6 1.0 reshape.75
  119.7 1.5 copy.77
  121.2 4.5 fusion.2
  125.7 1.3 copy.70
  127.9 227.7 %reduce-scatter.7.cloned.1.call-done = f32[16,4]{1,0:T(8,128)} async-done(((f32[512,4]{1,0:T(8,128)}), f32[16,4]{1,0:T(8,128)}) %reduce-scatter.7.cloned.1.call-update) | async-done | bytes 272
  355.6 0.8 reshape.76
  356.5 222.7 %reduce-scatter.5.cloned.1.call-done = f32[2,16,256]{2,1,0:T(8,128)} async-done(((f32[2,512,256]{2,1,0:T(8,128)}), f32[2,16,256]{2,1,0:T(8,128)}) %reduce-scatter.5.cloned.1.call-update) | async-done | bytes 32784 | tf_op jit(solution)/shard_map/reduce_scatter | solution.py:71
  579.2 84.4 %all-gather.5.cloned.1.call-done = bf16[256,4096]{1,0:T(8,128)(2,1)} async-done(((bf16[256,128]{1,0:T(8,128)(2,1)}), bf16[256,4096]{1,0:T(8,128)(2,1)}) %all-gather.5.cloned.1.call-update) | async-done | bytes 2097168 | tf_op jit(solution)/shard_map/all_gather | solution.py:81
  663.6 2.9 fusion.6
  666.6 21.4 %all-gather = bf16[16,1,256]{2,1,0:T(2,128)(2,1)S(1)} all-gather(bf16[1,1,256]{2,1,0:T(2,128)(2,1)S(1)} %reshape.66), channel_id=1, replica_groups=mesh['ctx'=32,'tp'=16] {'tp'}, dimensions={0}, use_global_device_ids=true | all-gather | bytes 8704 | tf_op jit(solution)/shard_map/all_gather | solution.py:88
  688.0 15.5 %all_gather.18 = bf16[2,16,4096]{2,1,0:T(8,128)(2,1)S(1)} all-gather(bf16[2,16,256]{2,1,0:T(8,128)(2,1)S(1)} %copy-done.2), channel_id=1, replica_groups=mesh['ctx'=32,'tp'=16] {'tp'}, dimensions={2}, use_global_device_ids=true | all-gather | bytes 278528 | tf_op jit(solution)/shard_map/all_gather | solution.py:87
  703.5 81.5 %all-reduce.3.cloned.1.call-done = f32[2,16,4096]{2,1,0:T(8,128)} async-done(((f32[2,16,4096]{2,1,0:T(8,128)}), f32[2,16,4096]{2,1,0:T(8,128)}) %all-reduce.3.cloned.1.call-update) | async-done | bytes 524304 | tf_op jit(solution)/shard_map/psum | solution.py:85
  785.0 1.2 multiply_reduce_fusion.1
  786.2 1.9 multiply_convert_fusion
  788.1 32.7 %all-gather.1 = s32[32,16,2]{1,2,0:T(2,128)S(1)} all-gather(s32[1,16,2]{1,2,0:T(2,128)S(1)} %bitcast.44), channel_id=1, replica_groups=mesh['ctx'=32,'tp'=16] {'ctx'}, dimensions={0}, use_global_device_ids=true | all-gather | bytes 4224 | tf_op jit(solution)/shard_map/all_gather | solution.py:49
  821.1 69.8 %all-gather.7.cloned.1.call-done = bf16[2,512,4096]{2,1,0:T(8,128)(2,1)} async-done(((bf16[2,16,4096]{2,1,0:T(8,128)(2,1)}), bf16[2,512,4096]{2,1,0:T(8,128)(2,1)}) %all-gather.7.cloned.1.call-update) | async-done | bytes 8388624 | tf_op jit(solution)/shard_map/all_gather | solution.py:97
  890.9 6.3 fusion.16
  897.2 96.8 %pmax.15 = f32[2,512]{1,0:T(2,128)S(1)} all-reduce(f32[2,512]{1,0:T(2,128)S(1)} %get-tuple-element.14), channel_id=1, replica_groups=mesh['ctx'=32,'tp'=16] {'ctx','tp'}, use_global_device_ids=true, to_apply=%region_8.9 | all-reduce | flops 1024 | bytes 8192 | tf_op jit(solution)/shard_map/pmax | solution.py:106
  994.1 95.3 %all-reduce = (f32[2,512]{1,0:T(2,128)S(1)}, f32[2,512]{1,0:T(2,128)S(1)}) all-reduce(f32[2,512]{1,0:T(2,128)S(1)} %get-tuple-element.3, f32[2,512]{1,0:T(2,128)S(1)} %get-tuple-element.2), channel_id=1, replica_groups=mesh['ctx'=32,'tp'=16] {'ctx','tp'}, use_global_device_ids=true, to_apply=%region_12.13 | all-reduce | flops 2048 | bytes 16384 | tf_op jit(solution)/shard_map/psum | solution.py:108
  (47 shorter events, 5.1 us)
Async XLA Ops:
  7.2 42.6 %copy-start = (bf16[2,1024,256]{2,1,0:T(8,128)(2,1)S(1)}, bf16[2,1024,256]{2,1,0:T(8,128)(2,1)}, u32[]{:S(2)}) copy-start(bf16[2,1024,256]{2,1,0:T(8,128)(2,1)} %param.13) | copy-start | bytes 3145732
  7.2 348.4 %reduce-scatter.7.cloned.1.call-start = ((), (), s32[]{:S(2)}) async-start(), calls=%async_computation.6 | async-start | bytes 270336
  119.7 459.5 %reduce-scatter.5.cloned.1.call-start = ((), (), s32[]{:S(2)}) async-start(), calls=%async_computation.2 | async-start | bytes 1081344 | tf_op jit(solution)/shard_map/reduce_scatter | solution.py:71
  121.2 545.3 %copy-start.5 = (bf16[256]{0:T(256)(128)(2,1)S(1)}, bf16[256]{0:T(256)(128)(2,1)}, u32[]{:S(2)}) copy-start(bf16[256]{0:T(256)(128)(2,1)} %param.17) | copy-start | bytes 1540
  121.2 566.8 %copy-start.2 = (bf16[2,16,256]{2,1,0:T(8,128)(2,1)S(1)}, bf16[2,16,256]{2,1,0:T(8,128)(2,1)}, u32[]{:S(2)}) copy-start(bf16[2,16,256]{2,1,0:T(8,128)(2,1)} %param.15) | copy-start | bytes 49156
  121.2 666.9 %copy-start.3 = (s32[2,16]{1,0:T(2,128)S(1)}, s32[2,16]{1,0:T(2,128)}, u32[]{:S(2)}) copy-start(s32[2,16]{1,0:T(2,128)} %param.19) | copy-start | bytes 388
  125.7 765.1 %copy-start.1 = (bf16[4096,128]{1,0:T(8,128)(2,1)S(1)}, bf16[4096,128]{1,0:T(8,128)(2,1)}, u32[]{:S(2)}) copy-start(bf16[4096,128]{1,0:T(8,128)(2,1)} %param.18) | copy-start | bytes 3145732
  127.1 962.4 %copy-start.4 = (s32[2]{0:T(128)S(1)}, s32[2]{0:T(128)}, u32[]{:S(2)}) copy-start(s32[2]{0:T(128)} %param.20) | copy-start | bytes 28
  127.1 963.2 %copy-start.6 = (s32[2]{0:T(128)S(1)}, s32[2]{0:T(128)}, u32[]{:S(2)}) copy-start(s32[2]{0:T(128)} %param.21) | copy-start | bytes 28
  127.1 536.5 %all-gather.5.cloned.1.call-start = ((), (), s32[]{:S(2)}) async-start(), calls=%async_computation.3 | async-start | bytes 2162688 | tf_op jit(solution)/shard_map/all_gather | solution.py:81
  127.8 657.1 %all-reduce.3.cloned.1.call-start = ((), (), s32[]{:S(2)}) async-start(), calls=%async_computation.4 | async-start | bytes 1048576 | tf_op jit(solution)/shard_map/psum | solution.py:85
  666.5 224.4 %all-gather.7.cloned.1.call-start = ((), (), s32[]{:S(2)}) async-start(), calls=%async_computation.5 | async-start | bytes 8650752 | tf_op jit(solution)/shard_map/all_gather | solution.py:97
Sparse Core Ops, SparseCore 0:
  119.8 235.7 reduce-scatter.6
  360.6 218.5 reduce-scatter.4
  582.7 80.8 all-gather.4
  666.6 118.3 all-reduce.2
  788.2 102.6 all-gather.6
where the time goes:
time: 1100 us
  waiting for transfers between devices  687 us (62%)
  blocking collectives  361 us (33%)
  matrix products  18.2 us (2%)
  between operations  15.8 us (1%)
    unnamed x6, waiting for transfers between devices  228 us
    reduce_scatter x1, waiting for transfers between devices, on_device(): lax.psum_scatter(softmax_numerator, 'ctx', scatter_dimension=1, tiled=True)  223 us
    pmax x1, blocking collectives, on_device(): global_peak = lax.pmax(local_peak, ('ctx', 'tp'))  96.8 us
    psum x1, blocking collectives, on_device(): exp_sum, target_logit = lax.psum((local_sum, picked), ('ctx', 'tp'))  95.3 us
    all_gather x1, waiting for transfers between devices, on_device(): lax.all_gather(out_proj, 'ctx', axis=1, tiled=True)  84.4 us
    psum x1, waiting for transfers between devices, on_device(): branch = lax.psum(branch_part, 'tp')  81.5 us
    all_gather x1, waiting for transfers between devices, on_device(): lax.all_gather(normed, 'ctx', axis=1, tiled=True)  69.8 us
    pmax x1, blocking collectives, on_device(): row_top = lax.pmax(local_top, 'ctx')  59.6 us
  transfers between devices with their start and end apart: 5, of which 5 were waited for; matrix products, arithmetic and copies ran while one was open for 1% of the time, Pallas kernels for 0%

commit v1 on v0

v1 whole, which is shorter than its diff:
```python
import functools
import math

import jax
import jax.numpy as jnp
from jax import lax
from jax.experimental import pallas as pl
from jax.experimental.pallas import tpu as pltpu
from jax.sharding import PartitionSpec as P

HEAD_SIZE = 128
ROPE_BASE = 500000.0
NORM_EPSILON = 1e-05
F32 = jnp.float32
BF16 = jnp.bfloat16


def near_first(n):
    return sorted(range(1, n), key=lambda d: (min(d, n - d), d))


def transposed(tiles):
    stacked = jnp.concatenate(tiles, axis=0)
    if stacked.shape[0] < 128:
        stacked = jnp.concatenate(
            [stacked, jnp.zeros((128 - stacked.shape[0], 128), F32)], axis=0
        )
    return stacked.T


def columns_to_tile(columns):
    rows = columns[0].shape[0]
    lane = lax.broadcasted_iota(jnp.int32, (rows, 128), 1)
    table = jnp.zeros((rows, 128), F32)
    for at, column in enumerate(columns):
        table = jnp.where(lane == at, column, table)
    if rows < 128:
        table = jnp.concatenate([table, jnp.zeros((128 - rows, 128), F32)], axis=0)
    return table.T[:8]


def merge(tiles):
    top = functools.reduce(jnp.maximum, tiles)
    weights = [jnp.exp(tile - top) for tile in tiles]
    total = functools.reduce(jnp.add, weights)
    return [weight / total for weight in weights], top + jnp.log(total)


def kernel(
    sizes,
    q, cosine, sine, target, resid, gain, keys_hbm, values_hbm, proj_hbm, head_hbm,
    out,
    keys, values, qbuf, obuf, ostat, xr, xs, yb, ystat, yr, ys, ab, rb, gs, gb, wo, wh,
    pb, cb, zs, zr, ez, ea, ex, ya, xa, lg, fz, fy, fx, fg,
    local_sem, send_sem, recv_sem,
):
    X, Y, Z = sizes
    S, R, W = q.shape
    heads = W // HEAD_SIZE
    ZH = Z // 2
    cols = pb.shape[-1]
    ctx, tp = lax.axis_index("ctx"), lax.axis_index("tp")
    x, y = ctx // Y, lax.rem(ctx, Y)
    z, k = tp // 2, lax.rem(tp, 2)
    zh, s_own = z // 2, lax.rem(z, 2)
    z_other = z + 1 - 2 * s_own

    def on_x(d):
        return (lax.rem(x + d + X, X) * Y + y, tp)

    def on_y(d):
        return (x * Y + lax.rem(y + d + Y, Y), tp)

    def on_z(d):
        return (ctx, lax.rem(z + d + Z, Z) * 2 + k)

    def on_pair(j):
        return (ctx, (z_other if j >= 2 else z) * 2 + (1 - k if j % 2 else k))

    started = []

    def copy_of(i, src, dst, device):
        return pltpu.make_async_remote_copy(
            src_ref=src,
            dst_ref=dst,
            send_sem=send_sem.at[i],
            recv_sem=recv_sem.at[i],
            device_id=device,
            device_id_type=pl.DeviceIdType.MESH,
        )

    def send(src, dst, device):
        copy = copy_of(len(started), src, dst, device)
        copy.start()
        started.append(copy)
        return len(started) - 1

    def recv(i, dst):
        copy_of(i, dst, dst, on_pair(1)).wait_recv()

    x_order, y_order, z_order = near_first(X), near_first(Y), near_first(Z)
    zh_order = near_first(ZH)

    barrier = pltpu.get_barrier_semaphore()
    peers = [on_y(d) for d in y_order] + [on_x(d) for d in x_order] + [on_z(d) for d in z_order]
    peers += [on_pair(1), on_pair(3)]
    for peer in peers:
        pl.semaphore_signal(
            barrier, inc=1, device_id=peer, device_id_type=pl.DeviceIdType.MESH
        )
    local = [
        pltpu.make_async_copy(keys_hbm, keys, local_sem.at[0]),
        pltpu.make_async_copy(values_hbm, values, local_sem.at[1]),
        pltpu.make_async_copy(proj_hbm, wo.at[y], local_sem.at[2]),
        pltpu.make_async_copy(head_hbm, wh.at[:, 0:128], local_sem.at[3]),
    ]
    for copy in local:
        copy.start()

    for s in range(S):
        for h in range(heads):
            at = slice(h * HEAD_SIZE, (h + 1) * HEAD_SIZE)
            part = q[s, :, at].astype(F32)
            turned = part * cosine[s] + pltpu.roll(part, HEAD_SIZE // 2, 1) * sine[s]
            qbuf[0, 0, s, :, at] = turned.astype(BF16)
    gs[k] = gain[...]
    rb[x] = resid[...]
    pl.semaphore_wait(barrier, len(peers))

    sent_y = {d: send(qbuf.at[0, 0], qbuf.at[0, d], on_y(d)) for d in y_order}
    sent_x = {}
    for e in x_order:
        sent_x[e, 0] = send(qbuf.at[0, 0], qbuf.at[e, 0], on_x(e))
    sent_gain = send(gs.at[k], gs.at[k], on_pair(1))
    local[3].wait()
    sent_head = {j: send(wh.at[:, 0:128], wh.at[:, j * 128 : (j + 1) * 128], on_pair(j)) for j in (2, 1)}
    for d in y_order:
        recv(sent_y[d], qbuf.at[0, d])
        for e in x_order:
            sent_x[e, d] = send(qbuf.at[0, d], qbuf.at[e, d], on_x(e))
    local[2].wait()
    sent_proj = {d: send(wo.at[y], wo.at[y], on_y(d)) for d in y_order}
    sent_resid = {e: send(rb.at[x], rb.at[x], on_x(e)) for e in x_order}

    scale = 1.0 / math.sqrt(HEAD_SIZE)
    group = Y * R

    def attend(e):
        logs = []
        for s in range(S):
            for h in range(heads):
                at = slice(h * HEAD_SIZE, (h + 1) * HEAD_SIZE)
                block = qbuf[e, :, s, :, at].reshape(group, HEAD_SIZE)
                scores = lax.dot_general(
                    block, keys[s, :, at], (((1,), (1,)), ((), ())), preferred_element_type=F32
                ) * scale
                top = jnp.max(scores, -1, keepdims=True)
                weights = jnp.exp(scores - top)
                total = jnp.sum(weights, -1, keepdims=True)
                summed = jnp.dot(
                    weights.astype(BF16), values[s, :, at], preferred_element_type=F32
                )
                obuf[e, s, :, at] = (summed / total).astype(BF16)
                logs.append(top + jnp.log(total))
        ostat[e] = columns_to_tile(logs)

    local[0].wait()
    local[1].wait()
    attend(0)
    recv(sent_gain, gs.at[1 - k])
    gb[z] = gs[...]
    sent_gains = {d: send(gs, gb.at[z], on_z(d)) for d in z_order}
    sent_o, sent_s = {}, {}
    for e in x_order:
        for d in [0] + y_order:
            recv(sent_x[e, d], qbuf.at[e, d])
        attend(e)
        sent_o[e] = send(obuf.at[e], xr.at[e], on_x(-e))
        sent_s[e] = send(ostat.at[e], xs.at[e], on_x(-e))
    for e in x_order:
        recv(sent_o[e], xr.at[e])
        recv(sent_s[e], xs.at[e])

    shares, log_sum = merge([ostat[0]] + [xs[e] for e in x_order])
    table = transposed(shares)
    for s in range(S):
        for h in range(heads):
            at = slice(h * HEAD_SIZE, (h + 1) * HEAD_SIZE)
            total = None
            for place, e in enumerate([0] + x_order):
                column = place * 8 + s * heads + h
                part = obuf[0, s, :, at] if e == 0 else xr[e, s, :, at]
                part = part.astype(F32) * table[:group, column : column + 1]
                total = part if total is None else total + part
            yb[:, s, :, at] = total.reshape(Y, R, HEAD_SIZE).astype(BF16)
    ystat[...] = log_sum
    sent_o, sent_s = {}, {}
    for d in y_order:
        sent_o[d] = send(yb.at[d], yr.at[d], on_y(-d))
        sent_s[d] = send(ystat, ys.at[d], on_y(-d))
    recv(sent_head[2], wh.at[:, 256:384])
    sent_head[3] = send(wh.at[:, 256:384], wh.at[:, 384:512], on_pair(1))
    for d in y_order:
        recv(sent_o[d], yr.at[d])
        recv(sent_s[d], ys.at[d])
    shares, _ = merge([ystat[...]] + [pltpu.roll(ys[d], 128 - d * R, 1) for d in y_order])
    table = transposed(shares)
    for s in range(S):
        for h in range(heads):
            at = slice(h * HEAD_SIZE, (h + 1) * HEAD_SIZE)
            total = None
            for place, d in enumerate([0] + y_order):
                column = place * 8 + s * heads + h
                part = yb[0, s, :, at] if d == 0 else yr[d, s, :, at]
                part = part.astype(F32) * table[:R, column : column + 1]
                total = part if total is None else total + part
            ab[x, s, :, at] = total.astype(BF16)

    sent = {e: send(ab.at[x], ab.at[x], on_x(e)) for e in x_order}
    for d in y_order:
        recv(sent_proj[d], wo.at[lax.rem(y - d + Y, Y)])
    for e in x_order:
        recv(sent_resid[e], rb.at[lax.rem(x - e + X, X)])
    for e in x_order:
        recv(sent[e], ab.at[lax.rem(x - e + X, X)])
    rows = X * S * R
    attended = ab[...].reshape(rows, W)
    residual = rb[...].reshape(rows, W).astype(F32)
    width = wo.shape[-1]
    for j in range(cols // W):
        if width < W:
            each = W // width
            weights = jnp.concatenate([wo[j * each + i] for i in range(each)], axis=1)
        else:
            first = j * W
            weights = wo[first // width, :, first % width : first % width + W]
        mine = (tp == x * (cols // W) + j).astype(F32)
        part = jnp.dot(attended, weights, preferred_element_type=F32) + residual * mine
        part = part.reshape(X * S, 2, R // 2, W)
        for half in range(2):
            pb[half, :, :, j * W : (j + 1) * W] = part[:, half]

    sent_core = send(pb.at[1 - k], cb, on_pair(1))
    recv(sent_core, cb)
    zs[...] = pb[k] + cb[...]
    sent = {d: send(zs.at[lax.rem(z + d, Z)], zr.at[d], on_z(d)) for d in z_order}
    for d in z_order:
        recv(sent_gains[d], gb.at[lax.rem(z - d + Z, Z)])
    stream = zs[z]
    for d in z_order:
        recv(sent[d], zr.at[d])
        stream = stream + zr[d]
    squares = jnp.sum(stream * stream, -1, keepdims=True)
    gains = [gb[x * (cols // W // 2) + j // 2, j % 2] for j in range(cols // W)]
    scaled = stream * jnp.concatenate(gains, axis=1)
    half = cols // 2
    ez[zh] = jnp.concatenate([scaled[:, :half], scaled[:, half:]], axis=0).astype(BF16)
    lane = lax.broadcasted_iota(jnp.int32, (R // 2, 128), 1)
    own_target = target[s_own, pl.ds(pl.multiple_of(k * (R // 2), R // 2), R // 2), :]
    own_target = own_target * (x == zh).astype(F32)
    ea[zh] = jnp.where(lane == 0, squares, jnp.where(lane == 1, own_target, 0.0))

    sent, sent_a = {}, {}
    for e in zh_order:
        sent[e] = send(ez.at[zh], ez.at[zh], on_z(2 * e))
        sent_a[e] = send(ea.at[zh], ea.at[zh], on_z(2 * e))
    for e in zh_order:
        recv(sent[e], ez.at[lax.rem(zh - e + ZH, ZH)])
        recv(sent_a[e], ea.at[lax.rem(zh - e + ZH, ZH)])
    unstacked = []
    for i in range(ZH):
        both = ez[i].astype(F32)
        unstacked.append(jnp.concatenate([both[: R // 2], both[R // 2 :]], axis=1))
    ex[x, y] = jnp.concatenate(unstacked, axis=0).astype(BF16)
    ya[y] = transposed([ea[i] for i in range(ZH)])[:8]
    sent = {d: send(ex.at[x, y], ex.at[x, y], on_y(d)) for d in y_order}
    sent_a = {d: send(ya.at[y], ya.at[y], on_y(d)) for d in y_order}
    sent_x = {}
    for e in x_order:
        sent_x[e, 0] = send(ex.at[x, y], ex.at[x, y], on_x(e))
    for d in y_order:
        from_y = lax.rem(y - d + Y, Y)
        recv(sent[d], ex.at[x, from_y])
        for e in x_order:
            sent_x[e, d] = send(ex.at[x, from_y], ex.at[x, from_y], on_x(e))
    for d in y_order:
        recv(sent_a[d], ya.at[lax.rem(y - d + Y, Y)])
    block = ZH * (R // 2)
    per_tile = 128 // block
    tiles = xa.shape[1]
    for i in range(tiles):
        total = None
        for place in range(min(per_tile, Y)):
            tile = ya[i * per_tile + place]
            if place:
                tile = pltpu.roll(tile, place * block, 1)
            total = tile if total is None else total + tile
        xa[x, i] = total
    sent_a = {e: send(xa.at[x], xa.at[x], on_x(e)) for e in x_order}

    recv(sent_head[1], wh.at[:, 128:256])
    recv(sent_head[3], wh.at[:, 384:512])
    slots = Y * block
    for e in [0] + x_order:
        from_x = lax.rem(x - e + X, X)
        if e:
            for d in [0] + y_order:
                recv(sent_x[e, d], ex.at[from_x, lax.rem(y - d + Y, Y)])
        part = jnp.dot(
            ex[from_x].reshape(slots, cols),
            wh[pl.ds(pl.multiple_of(from_x * cols, cols), cols), :],
            preferred_element_type=F32,
        )
        if e:
            lg[...] += part
        else:
            lg[...] = part
    for e in x_order:
        recv(sent_a[e], xa.at[lax.rem(x - e + X, X)])
    span = min(128, slots)
    for i in range(tiles):
        total = xa[0, i]
        for from_x in range(1, X):
            total = total + xa[from_x, i]
        table = transposed([lax.rsqrt(total * (1.0 / (X * cols)) + NORM_EPSILON), total])
        logits = lg[i * span : (i + 1) * span, :] * table[:span, 0:1]
        wanted = table[:span, 9:10]
        top = jnp.max(logits, -1, keepdims=True)
        sums = jnp.sum(jnp.exp(logits - top), -1, keepdims=True)
        lane = lax.broadcasted_iota(jnp.int32, (span, 128), 1)
        picked = jnp.zeros((span, 128), F32)
        for j in range(4):
            first = (ctx * (2 * Z) + on_pair(j)[1]) * 128
            hit = (lane + first).astype(F32) == wanted
            picked = picked + jnp.where(hit, logits[:, j * 128 : (j + 1) * 128], 0.0)
        fz[zh, i] = columns_to_tile(
            [top + jnp.log(sums), jnp.sum(picked, -1, keepdims=True)]
        )

    def combine(ref, count):
        parts = [ref[i] for i in range(count)]
        _, log_sum = merge(parts)
        row = lax.broadcasted_iota(jnp.int32, parts[0].shape, 1)
        return jnp.where(row == 0, log_sum, functools.reduce(jnp.add, parts))

    sent = {e: send(fz.at[zh], fz.at[zh], on_z(2 * e)) for e in zh_order}
    for e in zh_order:
        recv(sent[e], fz.at[lax.rem(zh - e + ZH, ZH)])
    fy[y] = combine(fz, ZH)
    sent = {d: send(fy.at[y], fy.at[y], on_y(d)) for d in y_order}
    for d in y_order:
        recv(sent[d], fy.at[lax.rem(y - d + Y, Y)])
    fx[x] = combine(fy, Y)
    sent = {e: send(fx.at[x], fx.at[x], on_x(e)) for e in x_order}
    for e in x_order:
        recv(sent[e], fx.at[lax.rem(x - e + X, X)])
    here = s_own * 2 + k
    fg[here] = combine(fx, X)
    sent = {j: send(fg.at[here], fg.at[here], on_pair(j)) for j in (1, 2, 3)}
    for j in (1, 2, 3):
        recv(sent[j], fg.at[(1 - s_own if j >= 2 else s_own) * 2 + (1 - k if j % 2 else k)])
    out[...] = fg[:, :, 0:1, :] - fg[:, :, 1:2, :]
    for copy in started:
        copy.wait_send()


def copies(X, Y, Z):
    x, y, z, zh = X - 1, Y - 1, Z - 1, Z // 2 - 1
    count = y + x + 1 + 2 + x * y + y + x + z + 2 * x + 2 * y + 1 + x + 1 + z
    return count + 2 * zh + 2 * y + x + x * y + x + zh + y + x + 3


def on_device(
    sizes,
    queries,
    positions,
    cached_keys,
    cached_values,
    residual_rows,
    out_proj,
    norm_gain,
    head_weight,
    targets,
    live_rows,
    mask_total,
):
    X, Y, Z = sizes
    S, R, W = queries.shape
    L = cached_keys.shape[1]
    D = head_weight.shape[0]
    cols = D // X
    ZH = Z // 2
    block = ZH * (R // 2)
    tiles = -(-Y * block // 128)
    frequency = ROPE_BASE ** (-2.0 * jnp.arange(HEAD_SIZE // 2, dtype=F32) / HEAD_SIZE)
    frequency = jnp.concatenate([frequency, frequency])
    sign = jnp.concatenate([-jnp.ones(HEAD_SIZE // 2, F32), jnp.ones(HEAD_SIZE // 2, F32)])
    angles = positions.astype(F32)[..., None] * frequency
    cosine, sine = jnp.cos(angles), jnp.sin(angles) * sign
    target = jnp.broadcast_to(targets.astype(F32)[..., None], (S, R, 128))
    gain = jnp.broadcast_to(norm_gain.astype(F32)[None], (8, W))
    vmem = pl.BlockSpec(memory_space=pltpu.VMEM)
    hbm = pl.BlockSpec(memory_space=pl.ANY)
    scratch = [
        ((S, L, W), BF16),
        ((S, L, W), BF16),
        ((X, Y, S, R, W), BF16),
        ((X, S, Y * R, W), BF16),
        ((X, 8, 128), F32),
        ((X, S, Y * R, W), BF16),
        ((X, 8, 128), F32),
        ((Y, S, R, W), BF16),
        ((8, 128), F32),
        ((Y, S, R, W), BF16),
        ((Y, 8, 128), F32),
        ((X, S, R, W), BF16),
        ((X, S, R, W), BF16),
        ((2, 8, W), F32),
        ((Z, 2, 8, W), F32),
        ((Y, W, out_proj.shape[1]), BF16),
        ((D, 4 * 128), BF16),
        ((2, Z, R // 2, cols), F32),
        ((Z, R // 2, cols), F32),
        ((Z, R // 2, cols), F32),
        ((Z, R // 2, cols), F32),
        ((ZH, R, cols // 2), BF16),
        ((ZH, R // 2, 128), F32),
        ((X, Y, block, cols), BF16),
        ((Y, 8, 128), F32),
        ((X, tiles, 8, 128), F32),
        ((Y * block, 4 * 128), F32),
        ((ZH, tiles, 8, 128), F32),
        ((Y, tiles, 8, 128), F32),
        ((X, tiles, 8, 128), F32),
        ((4, tiles, 8, 128), F32),
    ]
    count = copies(X, Y, Z)
    nll = pl.pallas_call(
        functools.partial(kernel, sizes),
        out_shape=jax.ShapeDtypeStruct((4, tiles, 1, 128), F32),
        in_specs=[vmem] * 6 + [hbm] * 4,
        out_specs=vmem,
        scratch_shapes=[pltpu.VMEM(*shape) for shape in scratch]
        + [
            pltpu.SemaphoreType.DMA((4,)),
            pltpu.SemaphoreType.DMA((count,)),
            pltpu.SemaphoreType.DMA((count,)),
        ],
        compiler_params=pltpu.CompilerParams(
            collective_id=0, has_side_effects=True, vmem_limit_bytes=44 * 1024 * 1024
        ),
        name="cloze",
    )(queries, cosine, sine, target, residual_rows, gain, cached_keys, cached_values, out_proj, head_weight)
    nll = nll.reshape(S, 2, -1, X, R // 2)[:, :, :Y]
    nll = jnp.transpose(nll, (0, 3, 2, 1, 4)).reshape(S, X * Y * R)
    alive = jnp.arange(X * Y * R, dtype=jnp.int32)[None, :] < live_rows[:, None]
    nll = jnp.where(alive, nll, 0.0)
    elbo_estimate = jnp.sum(jnp.sum(nll, 1) / mask_total.astype(F32)) / S
    token_nll = lax.dynamic_slice_in_dim(nll, lax.axis_index("ctx") * R, R, 1)
    return (token_nll, elbo_estimate)


def solution(mesh):
    Z = mesh.shape["tp"] // 2
    X = Z // 2
    sizes = (X, mesh.shape["ctx"] // X, Z)
    in_specs = (
        P(None, "ctx", "tp"),
        P(None, "ctx"),
        P(None, "ctx", "tp"),
        P(None, "ctx", "tp"),
        P(None, "ctx", "tp"),
        P("tp", "ctx"),
        P("tp"),
        P(None, ("ctx", "tp")),
        P(None, "ctx"),
        P(),
        P(),
    )
    return jax.shard_map(
        functools.partial(on_device, sizes),
        mesh=mesh,
        in_specs=in_specs,
        out_specs=(P(None, "ctx"), P()),
        check_vma=False,
    )
```

time: 1100 us -> 122 us (0.11)
  waiting for transfers between devices: 687 us -> 0 us
  blocking collectives: 361 us -> 0 us
  Pallas kernels: 0 us -> 108 us
  matrix products: 18.2 us -> 0 us
  between operations: 15.8 us -> 2.5 us
    unnamed x6 -> x0, waiting for transfers between devices: 228 us -> none
    reduce_scatter x1 -> x0, waiting for transfers between devices: 223 us -> none  [on_device(): lax.psum_scatter(softmax_numerator, 'ctx', scatter_dimension=1, tiled=True)]
    pmax x2 -> x0, blocking collectives: 156 us -> none  [the longest x1 96.8 us: on_device(): global_peak = lax.pmax(local_peak, ('ctx', 'tp'))]
    all_gather x2 -> x0, waiting for transfers between devices: 154 us -> none  [the longest x1 84.4 us: on_device(): lax.all_gather(out_proj, 'ctx', axis=1, tiled=True)]
    all_gather x4 -> x0, blocking collectives: 110 us -> none  [the longest x1 39.9 us: on_device(): lax.all_gather(rotated, 'ctx', axis=1, tiled=True)]
    pallas_call x0 -> x1, Pallas kernels: none -> 108 us  [on_device(): pl.pallas_call(functools.partial(kernel, sizes), out_shape=jax.ShapeDtype...]
    psum x1 -> x0, blocking collectives: 95.3 us -> none  [on_device(): exp_sum, target_logit = lax.psum((local_sum, picked), ('ctx', 'tp'))]
    psum x1 -> x0, waiting for transfers between devices: 81.5 us -> none  [on_device(): branch = lax.psum(branch_part, 'tp')]
  transfers between devices with their start and end apart: 5 -> 0, of which waited for: 5 -> 0; matrix products, arithmetic and copies ran while one was open for 1% -> 0% of each run, Pallas kernels for 0% -> 0%
where the time goes in v1:
time: 122 us
  Pallas kernels  108 us (89%)
  local copies, waits for them, and re-layouts  7.5 us (6%)
  other arithmetic  3.7 us (3%)
  between operations  2.5 us (2%)
    pallas_call x1, Pallas kernels, on_device(): pl.pallas_call(functools.partial(kernel, sizes), out_shape=jax.ShapeDtype...  108 us
    unnamed x18, local copies, waits for them, and re-layouts  5.95 us

profile of v1, /device:TPU:1, one launch (start us, length us, event | category | flops | bytes accessed | tf_op | source)
XLA Modules:
  0.0 121.7 jit_solution(5807236451276426850)
XLA Ops:
  0.6 0.0 copy-start.7
  0.7 0.1 pad_maximum_fusion
  0.7 0.7 convert_element_type.12
  1.4 0.7 convert_element_type.13
  2.1 0.7 broadcast_in_dim.10.gain
  2.8 0.1 broadcast_in_dim.9.target
  2.8 0.1 fusion
  3.0 0.6 copy-done.4
  3.6 1.2 %copy-done = bf16[2,1024,256]{2,1,0:T(8,128)(2,1)S(1)} copy-done((bf16[2,1024,256]{2,1,0:T(8,128)(2,1)S(1)}, bf16[2,1024,256]{2,1,0:T(8,128)(2,1)}, u32[]{:S(2)}) %copy-start) | copy-done | bytes 1048600
  4.8 1.2 %copy-done.1 = bf16[2,1024,256]{2,1,0:T(8,128)(2,1)S(1)} copy-done((bf16[2,1024,256]{2,1,0:T(8,128)(2,1)S(1)}, bf16[2,1024,256]{2,1,0:T(8,128)(2,1)}, u32[]{:S(2)}) %copy-start.1) | copy-done | bytes 1048600
  6.0 1.2 %copy-done.2 = bf16[4096,128]{1,0:T(8,128)(2,1)S(1)} copy-done((bf16[4096,128]{1,0:T(8,128)(2,1)S(1)}, bf16[4096,128]{1,0:T(8,128)(2,1)}, u32[]{:S(2)}) %copy-start.2) | copy-done | bytes 1048600
  7.2 0.7 copy-done.5
  8.0 108.0 %cloze.1 = f32[4,2,1,128]{3,2,1,0:T(1,128)S(1)} custom-call(bf16[2,16,256]{2,1,0:T(8,128)(2,1)S(1)} %copy-done.4, f32[2,16,128]{2,1,0:T(8,128)S(1)} %get-tuple-element.3.cosine, f32[2,16,128]{2,1,0:T(8,128)S(1)} %get-tuple-element.2.sine, f32[2,16,128]{2,1,0:T(8,128)S(1)} %broadcast_in_dim.9.target, bf16[2,16,256]{2,1,0:T(8,128)(2,1)S(1)} %copy-done.5, ...), custom_call_target="tpu_custom_call" | custom-call | tf_op jit(solution)/shard_map/cloze/pallas_call | solution.py:438
  116.0 0.5 broadcast.32
  116.5 0.7 reduce.4
  117.2 0.0 copy-start.6
  117.2 0.1 reshape.36
  117.3 0.5 copy-done.6
  117.8 0.2 select_reduce_fusion
  118.0 0.5 copy-done.8
  118.5 0.6 fusion.1
  119.7 0.1 copy.13
  119.8 0.1 reshape.37
  119.9 0.6 compare_select_fusion
  (11 shorter events, 0.0 us)
Async XLA Ops:
  0.6 2.2 %copy-start.7 = (f32[128]{0:T(128)S(1)}, f32[128]{0:T(128)}, u32[]{:S(2)}) copy-start(f32[128]{0:T(128)} %constant.22.clone.1) | copy-start | bytes 1540
  0.6 2.4 %copy-start.3 = (bf16[256,128]{1,0:T(8,128)(2,1)S(1)}, bf16[256,128]{1,0:T(8,128)(2,1)}, u32[]{:S(2)}) copy-start(bf16[256,128]{1,0:T(8,128)(2,1)} %proj_hbm.1) | copy-start | bytes 196612
  2.8 0.7 copy-start.4
  3.6 1.2 %copy-start = (bf16[2,1024,256]{2,1,0:T(8,128)(2,1)S(1)}, bf16[2,1024,256]{2,1,0:T(8,128)(2,1)}, u32[]{:S(2)}) copy-start(bf16[2,1024,256]{2,1,0:T(8,128)(2,1)} %keys_hbm.1) | copy-start | bytes 3145732
  4.8 1.2 %copy-start.1 = (bf16[2,1024,256]{2,1,0:T(8,128)(2,1)S(1)}, bf16[2,1024,256]{2,1,0:T(8,128)(2,1)}, u32[]{:S(2)}) copy-start(bf16[2,1024,256]{2,1,0:T(8,128)(2,1)} %values_hbm.1) | copy-start | bytes 3145732
  6.0 1.2 %copy-start.2 = (bf16[4096,128]{1,0:T(8,128)(2,1)S(1)}, bf16[4096,128]{1,0:T(8,128)(2,1)}, u32[]{:S(2)}) copy-start(bf16[4096,128]{1,0:T(8,128)(2,1)} %head_hbm.1) | copy-start | bytes 3145732
  7.2 0.7 copy-start.5
  117.2 0.7 copy-start.6
  117.8 0.7 copy-start.8

commit v2 on v1

v2 whole, which is shorter than its diff:
```python
import functools
import heapq
import math

import jax
import jax.numpy as jnp
from jax import lax
from jax.experimental import pallas as pl
from jax.experimental.pallas import tpu as pltpu
from jax.sharding import PartitionSpec as P

HEAD_SIZE = 128
ROPE_BASE = 500000.0
NORM_EPSILON = 1e-05
F32 = jnp.float32
BF16 = jnp.bfloat16


def near_first(n):
    return sorted(range(1, n), key=lambda d: (min(d, n - d), d))


def transposed(tiles):
    stacked = jnp.concatenate(tiles, axis=0)
    if stacked.shape[0] < 128:
        stacked = jnp.concatenate(
            [stacked, jnp.zeros((128 - stacked.shape[0], 128), F32)], axis=0
        )
    return stacked.T


def columns_to_tile(columns):
    rows = next(iter(columns.values())).shape[0]
    lane = lax.broadcasted_iota(jnp.int32, (rows, 128), 1)
    table = jnp.zeros((rows, 128), F32)
    for at, column in columns.items():
        table = jnp.where(lane == at, column, table)
    if rows < 128:
        table = jnp.concatenate([table, jnp.zeros((128 - rows, 128), F32)], axis=0)
    return table.T[:8]


def merge(tiles):
    top = functools.reduce(jnp.maximum, tiles)
    weights = [jnp.exp(tile - top) for tile in tiles]
    total = functools.reduce(jnp.add, weights)
    return [weight / total for weight in weights], top + jnp.log(total)


def kernel(
    sizes,
    live_rows, mask_total,
    q_hbm, positions_hbm, frequency_hbm, targets_hbm, resid_hbm, gain_hbm,
    keys_hbm, values_hbm, proj_hbm, head_hbm,
    out, loss,
    q, positions, frequency, targets, gain, keys, values, qbuf, obuf, ostat, xr, xs, yb, ystat, yr, ys, ab, rb, gs, gb, wo, wh,
    pb, cb, tt, zs, zr, ea, ex, ya, xa, lg, ft, fy, fx,
    local_sem, send_sem, recv_sem,
):
    X, Y, Z = sizes
    S, R, W = q_hbm.shape
    heads = W // HEAD_SIZE
    ZH = Z // 2
    cols = pb.shape[-1]
    ctx, tp = lax.axis_index("ctx"), lax.axis_index("tp")
    x, y = ctx // Y, lax.rem(ctx, Y)
    z, k = tp // 2, lax.rem(tp, 2)
    zh, s_own = z // 2, lax.rem(z, 2)
    z_other = z + 1 - 2 * s_own

    def on_x(d):
        return (lax.rem(x + d + X, X) * Y + y, tp)

    def on_y(d):
        return (x * Y + lax.rem(y + d + Y, Y), tp)

    def on_z(d):
        return (ctx, lax.rem(z + d + Z, Z) * 2 + k)

    def on_pair(j):
        return (ctx, (z_other if j >= 2 else z) * 2 + (1 - k if j % 2 else k))

    started = []

    def copy_of(i, src, dst, device):
        return pltpu.make_async_remote_copy(
            src_ref=src,
            dst_ref=dst,
            send_sem=send_sem.at[i],
            recv_sem=recv_sem.at[i],
            device_id=device,
            device_id_type=pl.DeviceIdType.MESH,
        )

    def send(src, dst, device):
        copy = copy_of(len(started), src, dst, device)
        copy.start()
        started.append(copy)
        return len(started) - 1

    def recv(i, dst):
        copy_of(i, dst, dst, on_pair(1)).wait_recv()

    def on_tp(d):
        return (ctx, lax.rem(tp + d, 2 * Z))

    x_order, y_order, z_order = near_first(X), near_first(Y), near_first(Z)
    zh_order = near_first(ZH)

    fetched = [
        (q_hbm, q), (positions_hbm, positions), (frequency_hbm, frequency),
        (head_hbm, wh.at[:, 0:128]), (targets_hbm, targets), (gain_hbm, gain),
        (resid_hbm, rb.at[x]), (keys_hbm, keys), (values_hbm, values), (proj_hbm, wo.at[y]),
    ]
    local = [
        pltpu.make_async_copy(src, dst, local_sem.at[i]) for i, (src, dst) in enumerate(fetched)
    ]
    for copy in local:
        copy.start()

    barrier = pltpu.get_barrier_semaphore()
    peers = [on_y(d) for d in y_order] + [on_x(d) for d in x_order]
    peers += [on_tp(d) for d in range(1, 2 * Z)]
    for peer in peers:
        pl.semaphore_signal(
            barrier, inc=1, device_id=peer, device_id_type=pl.DeviceIdType.MESH
        )

    def column_table(ref):
        table = jnp.concatenate([ref[...].astype(F32), jnp.zeros((S, 128 - R), F32)], axis=1)
        return transposed([jnp.concatenate([table, jnp.zeros((8 - S, 128), F32)], axis=0)])

    for copy in local[:3]:
        copy.wait()
    places = column_table(positions)
    lane = lax.broadcasted_iota(jnp.int32, (R, HEAD_SIZE), 1)
    for s in range(S):
        angles = places[:R, s : s + 1] * frequency[...]
        cosine, sine = jnp.cos(angles), jnp.sin(angles)
        sine = jnp.where(lane < HEAD_SIZE // 2, -sine, sine)
        for h in range(heads):
            at = slice(h * HEAD_SIZE, (h + 1) * HEAD_SIZE)
            part = q[s, :, at].astype(F32)
            turned = part * cosine + pltpu.roll(part, HEAD_SIZE // 2, 1) * sine
            qbuf[0, 0, s, :, at] = turned.astype(BF16)
    for copy in local[3:6]:
        copy.wait()
    gs[k] = jnp.broadcast_to(gain[...].astype(F32).reshape(1, W), (8, W))
    wanted = column_table(targets)
    for s in range(S):
        tt[s] = jnp.broadcast_to(wanted[:R, s : s + 1], (R, 128))
    pl.semaphore_wait(barrier, len(peers))

    sent_y = {d: send(qbuf.at[0, 0], qbuf.at[0, d], on_y(d)) for d in y_order}
    sent_x = {}
    sides = {1: [], 2: [1]}.get(X, [1, X - 1])
    for e in sides:
        sent_x[e, 0] = send(qbuf.at[0, 0], qbuf.at[e, 0], on_x(e))
    sent_gain = send(gs.at[k], gs.at[k], on_pair(1))
    sent_head = {j: send(wh.at[:, 0:128], wh.at[:, j * 128 : (j + 1) * 128], on_pair(j)) for j in (2, 1)}
    for d in y_order:
        recv(sent_y[d], qbuf.at[0, d])
        for e in sides:
            sent_x[e, d] = send(qbuf.at[0, d], qbuf.at[e, d], on_x(e))
    for e in x_order[len(sides) :]:
        for d in [0] + y_order:
            sent_x[e, d] = send(qbuf.at[0, d], qbuf.at[e, d], on_x(e))
    for copy in local[6:]:
        copy.wait()
    sent_proj = {d: send(wo.at[y], wo.at[y], on_y(d)) for d in y_order}
    sent_resid = {e: send(rb.at[x], rb.at[x], on_x(e)) for e in x_order}

    scale = math.log2(math.e) / math.sqrt(HEAD_SIZE)
    group = Y * R

    def attend(e, s):
        logs = {}
        for h in range(heads):
            at = slice(h * HEAD_SIZE, (h + 1) * HEAD_SIZE)
            block = qbuf[e, :, s, :, at].reshape(group, HEAD_SIZE)
            scores = lax.dot_general(
                block, keys[s, :, at], (((1,), (1,)), ((), ())), preferred_element_type=F32
            )
            top = jnp.max(scores, -1, keepdims=True)
            weights = jnp.exp2((scores - top) * scale)
            total = jnp.sum(weights, -1, keepdims=True)
            summed = jnp.dot(
                weights.astype(BF16), values[s, :, at], preferred_element_type=F32
            )
            obuf[e, s, :, at] = (summed / total).astype(BF16)
            logs[s * heads + h] = top * (1.0 / math.sqrt(HEAD_SIZE)) + jnp.log(total)
        ostat[e, s] = columns_to_tile(logs)

    for s in range(S):
        attend(0, s)
    recv(sent_gain, gs.at[1 - k])
    gb[z] = gs[...]
    sent_gains = {d: send(gs, gb.at[z], on_z(d)) for d in z_order}
    sent_o, sent_s = {}, {}
    units = [(e, s) for s in range(S) for e in sides]
    for e, s in units + [(e, s) for e in x_order[len(sides) :] for s in range(S)]:
        if s == 0:
            for d in [0] + y_order:
                recv(sent_x[e, d], qbuf.at[e, d])
        attend(e, s)
        sent_o[e, s] = send(obuf.at[e, s], xr.at[e, s], on_x(-e))
        sent_s[e, s] = send(ostat.at[e, s], xs.at[e, s], on_x(-e))

    sent_yo, sent_ys, log_sums = {}, {}, []
    for s in range(S):
        for e in x_order:
            recv(sent_o[e, s], xr.at[e, s])
            recv(sent_s[e, s], xs.at[e, s])
        shares, log_sum = merge([ostat[0, s]] + [xs[e, s] for e in x_order])
        log_sums.append(log_sum)
        table = transposed(shares)
        for h in range(heads):
            at = slice(h * HEAD_SIZE, (h + 1) * HEAD_SIZE)
            total = None
            for place, e in enumerate([0] + x_order):
                column = place * 8 + s * heads + h
                part = obuf[0, s, :, at] if e == 0 else xr[e, s, :, at]
                part = part.astype(F32) * table[:group, column : column + 1]
                total = part if total is None else total + part
            yb[s, :, :, at] = total.reshape(Y, R, HEAD_SIZE).astype(BF16)
        for d in y_order:
            sent_yo[d, s] = send(yb.at[s, d], yr.at[s, d], on_y(-d))
    row = lax.broadcasted_iota(jnp.int32, (8, 128), 0)
    ystat[...] = jnp.where(row < heads, log_sums[0], log_sums[1])
    for d in y_order:
        sent_ys[d] = send(ystat, ys.at[d], on_y(-d))
    for d in y_order:
        recv(sent_ys[d], ys.at[d])
    shares, _ = merge([ystat[...]] + [pltpu.roll(ys[d], 128 - d * R, 1) for d in y_order])
    table = transposed(shares)
    for s in range(S):
        for d in y_order:
            recv(sent_yo[d, s], yr.at[s, d])
        for h in range(heads):
            at = slice(h * HEAD_SIZE, (h + 1) * HEAD_SIZE)
            total = None
            for place, d in enumerate([0] + y_order):
                column = place * 8 + s * heads + h
                part = yb[s, 0, :, at] if d == 0 else yr[s, d, :, at]
                part = part.astype(F32) * table[:R, column : column + 1]
                total = part if total is None else total + part
            ab[x, s, :, at] = total.astype(BF16)

    sent = {e: send(ab.at[x], ab.at[x], on_x(e)) for e in x_order}
    for d in y_order:
        recv(sent_proj[d], wo.at[lax.rem(y - d + Y, Y)])
    for e in x_order:
        recv(sent_resid[e], rb.at[lax.rem(x - e + X, X)])
    for e in x_order:
        recv(sent[e], ab.at[lax.rem(x - e + X, X)])
    rows = X * S * R
    attended = ab[...].reshape(rows, W)
    residual = rb[...].reshape(rows, W).astype(F32)
    width = wo.shape[-1]
    for j in range(cols // W):
        if width < W:
            each = W // width
            weights = jnp.concatenate([wo[j * each + i] for i in range(each)], axis=1)
        else:
            first = j * W
            weights = wo[first // width, :, first % width : first % width + W]
        mine = (tp == x * (cols // W) + j).astype(F32)
        part = jnp.dot(attended, weights, preferred_element_type=F32) + residual * mine
        part = part.reshape(X * S, 2, R // 2, W)
        for half in range(2):
            pb[half, :, :, j * W : (j + 1) * W] = part[:, half]

    eight, half = R // 2, cols // 2
    sent_core = send(pb.at[1 - k], cb, on_pair(1))
    recv(sent_core, cb)
    summed = pb[k] + cb[...]
    zs[...] = jnp.concatenate([summed[:, :, :half], summed[:, :, half:]], axis=1).astype(BF16)
    sent = {d: send(zs.at[lax.rem(z + d, Z)], zr.at[d], on_z(d)) for d in z_order}
    for d in z_order:
        recv(sent_gains[d], gb.at[lax.rem(z - d + Z, Z)])
    stream = pb[k, z] + cb[z]
    for d in z_order:
        recv(sent[d], zr.at[d])
        both = zr[d].astype(F32)
        stream = stream + jnp.concatenate([both[:eight], both[eight:]], axis=1)
    gains = [gb[x * (cols // W // 2) + j // 2, j % 2] for j in range(cols // W)]
    scaled = stream * jnp.concatenate(gains, axis=1)
    ex[x, y, zh] = jnp.concatenate([scaled[:, :half], scaled[:, half:]], axis=0).astype(BF16)

    def near(e):
        return lax.rem(zh - e + ZH, ZH)

    def piece(i, d, e):
        return ex.at[lax.rem(x - i + X, X), lax.rem(y - d + Y, Y), near(e)]

    y_direct = [d for d in y_order if Y < 8 or min(d, Y - d) <= 2]
    z_steps = [0] + zh_order
    under_way, busy = [], {}

    def launch(now, axis, step, i, d, e):
        size = {"x": X, "y": Y, "z": ZH}[axis]
        device = {"x": on_x, "y": on_y, "z": lambda n: on_z(2 * n)}[axis](step)
        number = send(piece(i, d, e), piece(i, d, e), device)
        way = step % size
        way = way if 2 * way <= size else way - size
        link = (axis, way > 0)
        busy[link] = max(now, busy.get(link, 0.0)) + 0.35 * abs(way)
        there = [i, d, e]
        at = "xyz".index(axis)
        there[at] = (there[at] + step) % size
        hops = abs(way) * (2 if axis == "z" else 1)
        heapq.heappush(under_way, (busy[link] + 1.4 + 0.7 * hops, number, tuple(there)))

    def spread_y(now, i, d, e):
        if d == 0:
            for step in y_direct:
                launch(now, "y", step, i, d, e)
        elif Y == 8 and d in (2, Y - 2):
            step = 1 if d == 2 else -1
            launch(now, "y", step, i, d, e)
            if (i + e + (step > 0)) % 2:
                launch(now, "y", 2 * step, i, d, e)

    def arrived(now, i, d, e):
        if e == 0 or i == 0:
            spread_y(now, i, d, e)
        if e and i == 0:
            for step in sides:
                launch(now, "x", step, i, d, e)
        elif e and X == 4 and i == (1 if (z_steps.index(e) + d) % 2 else X - 1):
            launch(now, "x", 1 if i == 1 else -1, i, d, e)

    for e in zh_order:
        launch(0.0, "z", e, 0, 0, 0)
    for i in x_order:
        launch(0.0, "x", i, 0, 0, 0)
    spread_y(0.0, 0, 0, 0)
    lane = lax.broadcasted_iota(jnp.int32, (eight, 128), 1)
    squares = jnp.sum(stream * stream, -1, keepdims=True)
    wanted = tt[s_own, pl.ds(pl.multiple_of(k * eight, eight), eight), :] * (x == zh).astype(F32)
    ea[zh] = jnp.where(lane == 0, squares, jnp.where(lane == 1, wanted, 0.0))
    sent_az = {e: send(ea.at[zh], ea.at[zh], on_z(2 * e)) for e in zh_order}
    recv(sent_head[2], wh.at[:, 256:384])
    sent_head[3] = send(wh.at[:, 256:384], wh.at[:, 384:512], on_pair(1))

    block = ZH * eight
    per_tile = 128 // block
    tiles = xa.shape[1]
    sent_ay, sent_ax = {}, {}

    def rows_along_y():
        for e in zh_order:
            recv(sent_az[e], ea.at[near(e)])
        ya[y] = transposed([ea[i] for i in range(ZH)])[:8]
        for d in y_order:
            sent_ay[d] = send(ya.at[y], ya.at[y], on_y(d))

    def rows_along_x():
        for d in y_order:
            recv(sent_ay[d], ya.at[lax.rem(y - d + Y, Y)])
        for i in range(tiles):
            total = None
            for place in range(min(per_tile, Y)):
                tile = ya[i * per_tile + place]
                if place:
                    tile = pltpu.roll(tile, place * block, 1)
                total = tile if total is None else total + tile
            xa[x, i] = total
        for e in x_order:
            sent_ax[e] = send(xa.at[x], xa.at[x], on_x(e))

    slots = Y * ZH * eight

    def multiply(i):
        if not complete:
            for j in (1, 3):
                recv(sent_head[j], wh.at[:, j * 128 : (j + 1) * 128])
        from_x = lax.rem(x - i + X, X)
        block = ex[from_x].reshape(Y * ZH * R, half)
        total = None
        for upper in range(2):
            start = pl.multiple_of(from_x * cols + upper * half, half)
            part = jnp.dot(block, wh[pl.ds(start, half), :], preferred_element_type=F32)
            part = part.reshape(Y * ZH, 2, eight, 4 * 128)[:, upper]
            total = part if total is None else total + part
        total = total.reshape(slots, 4 * 128)
        if complete:
            lg[...] += total
        else:
            lg[...] = total
        complete.append(i)

    complete = []
    missing = {i: Y * ZH for i in range(X)}
    missing[0] -= 1
    later = [(6.0, rows_along_y), (11.0, rows_along_x)]
    while under_way:
        now, number, place = heapq.heappop(under_way)
        while later and later[0][0] < now:
            later.pop(0)[1]()
        recv(number, piece(*place))
        arrived(now, *place)
        missing[place[0]] -= 1
        if missing[place[0]] == 0 and under_way:
            multiply(place[0])
    for _, step in later:
        step()
    for i in range(X):
        if i not in complete:
            multiply(i)
    for e in x_order:
        recv(sent_ax[e], xa.at[lax.rem(x - e + X, X)])
    span = min(128, slots)
    fin = None
    for i in range(tiles):
        total = xa[0, i]
        for from_x in range(1, X):
            total = total + xa[from_x, i]
        table = transposed([lax.rsqrt(total * (1.0 / (X * cols)) + NORM_EPSILON), total])
        logits = lg[i * span : (i + 1) * span, :] * table[:span, 0:1]
        wanted = table[:span, 9:10]
        top = jnp.max(logits, -1, keepdims=True)
        sums = jnp.sum(jnp.exp(logits - top), -1, keepdims=True)
        lane = lax.broadcasted_iota(jnp.int32, (span, 128), 1)
        picked = jnp.zeros((span, 128), F32)
        for j in range(4):
            first = (ctx * (2 * Z) + on_pair(j)[1]) * 128
            hit = (lane + first).astype(F32) == wanted
            picked = picked + jnp.where(hit, logits[:, j * 128 : (j + 1) * 128], 0.0)
        tile = columns_to_tile(
            {i: top + jnp.log(sums), 4 + i: jnp.sum(picked, -1, keepdims=True)}
        )
        fin = tile if fin is None else fin + tile
    ft[tp] = fin

    def combine(parts):
        _, log_sum = merge(parts)
        row = lax.broadcasted_iota(jnp.int32, (8, 128), 0)
        return jnp.where(row < 4, log_sum, functools.reduce(jnp.add, parts))

    sent = {d: send(ft.at[tp], ft.at[tp], on_tp(d)) for d in range(1, 2 * Z)}
    for d in range(1, 2 * Z):
        recv(sent[d], ft.at[lax.rem(tp - d + 2 * Z, 2 * Z)])
    for s in range(S):
        first, second = (
            combine([ft[4 * i + 2 * s + core] for i in range(ZH)]) for core in range(2)
        )
        fy[y, s] = jnp.where(lax.rem(row, 4) < 2, first, pltpu.roll(second, 2, 0))
    sent = {d: send(fy.at[y], fy.at[y], on_y(d)) for d in y_order}
    for d in y_order:
        recv(sent[d], fy.at[lax.rem(y - d + Y, Y)])
    for s in range(S):
        fx[x, s] = combine([fy[i, s] for i in range(Y)])
    sent = {e: send(fx.at[x], fx.at[x], on_x(e)) for e in x_order}
    for e in x_order:
        recv(sent[e], fx.at[lax.rem(x - e + X, X)])

    lane = lax.broadcasted_iota(jnp.int32, (8, 128), 1)
    from_y = lax.rem(row, 2) * per_tile + lane // block
    from_x = lax.rem(lane, block) // eight
    slot = (from_x * Y + from_y) * R + (row // 2) * eight + lax.rem(lane, eight)
    counted = (row < 4) & (from_y < Y)
    sample_sum, own = None, []
    first = lax.rem(y, per_tile) * block + x * eight
    member = lax.broadcasted_iota(jnp.int32, (R, 128), 0)
    place = lax.broadcasted_iota(jnp.int32, (R, 128), 1) == first + lax.rem(member, eight)
    for s in range(S):
        tile = combine([fx[i, s] for i in range(X)])
        tile = tile - pltpu.roll(tile, 4, 0)
        tile = jnp.where(counted & (slot < live_rows[s]), tile, 0.0)
        total = jnp.sum(jnp.sum(tile, 1, keepdims=True), 0, keepdims=True)
        total = total / jnp.full((1, 1), mask_total[s], jnp.int32).astype(F32)
        sample_sum = total if sample_sum is None else sample_sum + total
        in_first = y < per_tile
        lower = jnp.where(in_first, tile[0:1], tile[1:2])
        upper = jnp.where(in_first, tile[2:3], tile[3:4])
        own.append(jnp.where(place, jnp.where(member < eight, lower, upper), 0.0))
    loss[...] = sample_sum * (1.0 / S)
    token = jnp.sum(transposed(own), 0, keepdims=True)
    for s in range(S):
        out[s : s + 1, :] = token[:, s * R : (s + 1) * R]
    for copy in started:
        copy.wait_send()
    assert len(started) == copies(X, Y, Z), len(started)


def copies(X, Y, Z):
    x, y, z, zh = X - 1, Y - 1, Z - 1, Z // 2 - 1
    count = y + x + 1 + 2 + x * y + y + x + z + 4 * x + 3 * y + x + 1 + z
    count += X * Y * Z // 2 - 1 + 1 + zh + y + x
    return count + 2 * Z - 1 + y + x


def on_device(
    sizes,
    queries,
    positions,
    cached_keys,
    cached_values,
    residual_rows,
    out_proj,
    norm_gain,
    head_weight,
    targets,
    live_rows,
    mask_total,
):
    X, Y, Z = sizes
    S, R, W = queries.shape
    L = cached_keys.shape[1]
    D = head_weight.shape[0]
    cols = D // X
    ZH = Z // 2
    block = ZH * (R // 2)
    tiles = -(-Y * block // 128)
    frequency = ROPE_BASE ** (-2.0 * jnp.arange(HEAD_SIZE // 2, dtype=F32) / HEAD_SIZE)
    frequency = jnp.concatenate([frequency, frequency])[None]
    vmem = pl.BlockSpec(memory_space=pltpu.VMEM)
    hbm = pl.BlockSpec(memory_space=pl.ANY)
    scratch = [
        ((S, R, W), BF16),
        ((S, R), jnp.int32),
        ((1, HEAD_SIZE), F32),
        ((S, R), jnp.int32),
        ((W,), BF16),
        ((S, L, W), BF16),
        ((S, L, W), BF16),
        ((X, Y, S, R, W), BF16),
        ((X, S, Y * R, W), BF16),
        ((X, S, 8, 128), F32),
        ((X, S, Y * R, W), BF16),
        ((X, S, 8, 128), F32),
        ((S, Y, R, W), BF16),
        ((8, 128), F32),
        ((S, Y, R, W), BF16),
        ((Y, 8, 128), F32),
        ((X, S, R, W), BF16),
        ((X, S, R, W), BF16),
        ((2, 8, W), F32),
        ((Z, 2, 8, W), F32),
        ((Y, W, out_proj.shape[1]), BF16),
        ((D, 4 * 128), BF16),
        ((2, Z, R // 2, cols), F32),
        ((Z, R // 2, cols), F32),
        ((S, R, 128), F32),
        ((Z, R, cols // 2), BF16),
        ((Z, R, cols // 2), BF16),
        ((ZH, R // 2, 128), F32),
        ((X, Y, ZH, R, cols // 2), BF16),
        ((Y, 8, 128), F32),
        ((X, tiles, 8, 128), F32),
        ((Y * block, 4 * 128), F32),
        ((2 * Z, 8, 128), F32),
        ((Y, S, 8, 128), F32),
        ((X, S, 8, 128), F32),
    ]
    count = copies(X, Y, Z)
    smem = pl.BlockSpec(memory_space=pltpu.SMEM)
    token_nll, loss = pl.pallas_call(
        functools.partial(kernel, sizes),
        out_shape=[jax.ShapeDtypeStruct((S, R), F32), jax.ShapeDtypeStruct((1, 1), F32)],
        in_specs=[smem] * 2 + [hbm] * 10,
        out_specs=[vmem, vmem],
        scratch_shapes=[pltpu.VMEM(*shape) for shape in scratch]
        + [
            pltpu.SemaphoreType.DMA((10,)),
            pltpu.SemaphoreType.DMA((count,)),
            pltpu.SemaphoreType.DMA((count,)),
        ],
        compiler_params=pltpu.CompilerParams(
            collective_id=0, has_side_effects=True, vmem_limit_bytes=60 * 1024 * 1024
        ),
        name="cloze",
    )(
        live_rows, mask_total, queries, positions, frequency, targets, residual_rows,
        norm_gain, cached_keys, cached_values, out_proj, head_weight,
    )
    return (token_nll, loss.reshape(()))


def solution(mesh):
    Z = mesh.shape["tp"] // 2
    X = Z // 2
    sizes = (X, mesh.shape["ctx"] // X, Z)
    in_specs = (
        P(None, "ctx", "tp"),
        P(None, "ctx"),
        P(None, "ctx", "tp"),
        P(None, "ctx", "tp"),
        P(None, "ctx", "tp"),
        P("tp", "ctx"),
        P("tp"),
        P(None, ("ctx", "tp")),
        P(None, "ctx"),
        P(),
        P(),
    )
    return jax.shard_map(
        functools.partial(on_device, sizes),
        mesh=mesh,
        in_specs=in_specs,
        out_specs=(P(None, "ctx"), P()),
        check_vma=False,
    )
```

time: 122 us -> 102 us (0.84)
  Pallas kernels: 108 us -> 97.6 us
  local copies, waits for them, and re-layouts: 7.5 us -> 1.21 us
  other arithmetic: 3.7 us -> 0.6 us
    pallas_call x1, Pallas kernels: 108 us -> 97.6 us  [on_device(): pl.pallas_call(functools.partial(kernel, sizes), out_shape=[jax.ShapeDtyp...]
    unnamed x18 -> x3, local copies, waits for them, and re-layouts: 5.95 us -> 1.21 us
    convert_element_type x2 -> x0, other arithmetic: 1.37 us -> none  [the longest x1 0.68 us: on_device(): angles = positions.astype(F32)[..., None] * frequency]
where the time goes in v2:
time: 102 us
  Pallas kernels  97.6 us (96%)
  between operations  2.41 us (2%)
  local copies, waits for them, and re-layouts  1.21 us (1%)
    pallas_call x1, Pallas kernels, on_device(): pl.pallas_call(functools.partial(kernel, sizes), out_shape=[jax.ShapeDtyp...  97.6 us

profile of v2, /device:TPU:1, one launch (start us, length us, event | category | flops | bytes accessed | tf_op | source)
XLA Modules:
  0.0 101.8 jit_solution(600547223759737889)
XLA Ops:
  0.6 0.6 maximum_bitcast_fusion.frequency_hbm
  1.2 97.6 %cloze.1 = (f32[2,16]{1,0:T(2,128)}, f32[1,1]{1,0:T(1,128)}) custom-call(s32[2]{0:T(128)} %live_rows.1, s32[2]{0:T(128)} %mask_total.1, bf16[2,16,256]{2,1,0:T(8,128)(2,1)} %q_hbm.1, s32[2,16]{1,0:T(2,128)} %positions_hbm.1, f32[1,128]{1,0:T(1,128)} %maximum_bitcast_fusion.frequency_hbm, s32[2,16]{1,0:T(2,128)} %targets_hbm.1, ...), custom_call_target="tpu_custom_call" | custom-call | tf_op jit(solution)/shard_map/cloze/pallas_call | solution.py:559
  98.8 0.0 copy-start
  98.8 0.6 copy-done
  99.5 0.6 copy.15
  (1 shorter events, 0.0 us)
Async XLA Ops:
  98.8 0.7 copy-start

commit v3 on v2

--- a/solution.py
+++ b/solution.py
@@ -49,24 +49,23 @@
 
 def kernel(
     sizes,
-    live_rows, mask_total,
-    q_hbm, positions_hbm, frequency_hbm, targets_hbm, resid_hbm, gain_hbm,
+    live_hbm, mask_hbm, q_hbm, positions_hbm, targets_hbm, resid_hbm, gain_hbm,
     keys_hbm, values_hbm, proj_hbm, head_hbm,
     out, loss,
-    q, positions, frequency, targets, gain, keys, values, qbuf, obuf, ostat, xr, xs, yb, ystat, yr, ys, ab, rb, gs, gb, wo, wh,
-    pb, cb, tt, zs, zr, ea, ex, ya, xa, lg, ft, fy, fx,
+    live_rows, mask_total, q, positions, targets, resid, gain, keys, values, qbuf, obuf, ostat,
+    xr, xs, yb, ystat, yr, ys, ab, at_x, rb, gs, gb, wo, wh, own, tt, zs, zr, ea, ex, ya, xa, lg, ft, fy, fx,
     local_sem, send_sem, recv_sem,
 ):
     X, Y, Z = sizes
     S, R, W = q_hbm.shape
     heads = W // HEAD_SIZE
     ZH = Z // 2
-    cols = pb.shape[-1]
+    cols = own.shape[-1]
     ctx, tp = lax.axis_index("ctx"), lax.axis_index("tp")
     x, y = ctx // Y, lax.rem(ctx, Y)
     z, k = tp // 2, lax.rem(tp, 2)
-    zh, s_own = z // 2, lax.rem(z, 2)
-    z_other = z + 1 - 2 * s_own
+    zh, parity = z // 2, lax.rem(z, 2)
+    z_other = z + 1 - 2 * parity
 
     def on_x(d):
         return (lax.rem(x + d + X, X) * Y + y, tp)
@@ -104,13 +103,17 @@
     def on_tp(d):
         return (ctx, lax.rem(tp + d, 2 * Z))
 
+    def other_core(device):
+        return (device[0], z * 2 + 1 - k)
+
     x_order, y_order, z_order = near_first(X), near_first(Y), near_first(Z)
     zh_order = near_first(ZH)
 
     fetched = [
-        (q_hbm, q), (positions_hbm, positions), (frequency_hbm, frequency),
+        (positions_hbm, positions), (q_hbm, q),
         (head_hbm, wh.at[:, 0:128]), (targets_hbm, targets), (gain_hbm, gain),
-        (resid_hbm, rb.at[x]), (keys_hbm, keys), (values_hbm, values), (proj_hbm, wo.at[y]),
+        (live_hbm, live_rows), (mask_hbm, mask_total),
+        (resid_hbm, resid), (keys_hbm, keys), (values_hbm, values), (proj_hbm, wo.at[k, y]),
     ]
     local = [
         pltpu.make_async_copy(src, dst, local_sem.at[i]) for i, (src, dst) in enumerate(fetched)
@@ -121,6 +124,7 @@
     barrier = pltpu.get_barrier_semaphore()
     peers = [on_y(d) for d in y_order] + [on_x(d) for d in x_order]
     peers += [on_tp(d) for d in range(1, 2 * Z)]
+    peers += [other_core(on_x(d)) for d in x_order]
     for peer in peers:
         pl.semaphore_signal(
             barrier, inc=1, device_id=peer, device_id_type=pl.DeviceIdType.MESH
@@ -130,20 +134,23 @@
         table = jnp.concatenate([ref[...].astype(F32), jnp.zeros((S, 128 - R), F32)], axis=1)
         return transposed([jnp.concatenate([table, jnp.zeros((8 - S, 128), F32)], axis=0)])
 
-    for copy in local[:3]:
-        copy.wait()
+    lane = lax.broadcasted_iota(jnp.int32, (R, HEAD_SIZE), 1)
+    place = lax.rem(lane, HEAD_SIZE // 2).astype(F32)
+    frequency = ROPE_BASE ** (-2.0 * place / HEAD_SIZE)
+    local[0].wait()
     places = column_table(positions)
-    lane = lax.broadcasted_iota(jnp.int32, (R, HEAD_SIZE), 1)
-    for s in range(S):
-        angles = places[:R, s : s + 1] * frequency[...]
-        cosine, sine = jnp.cos(angles), jnp.sin(angles)
+    angles = [places[:R, s : s + 1] * frequency for s in range(S)]
+    turns = [(jnp.cos(angle), jnp.sin(angle)) for angle in angles]
+    local[1].wait()
+    for s in range(S):
+        cosine, sine = turns[s]
         sine = jnp.where(lane < HEAD_SIZE // 2, -sine, sine)
         for h in range(heads):
             at = slice(h * HEAD_SIZE, (h + 1) * HEAD_SIZE)
             part = q[s, :, at].astype(F32)
             turned = part * cosine + pltpu.roll(part, HEAD_SIZE // 2, 1) * sine
-            qbuf[0, 0, s, :, at] = turned.astype(BF16)
-    for copy in local[3:6]:
+            qbuf[s, 0, 0, :, at] = turned.astype(BF16)
+    for copy in local[2:5]:
         copy.wait()
     gs[k] = jnp.broadcast_to(gain[...].astype(F32).reshape(1, W), (8, W))
     wanted = column_table(targets)
@@ -151,35 +158,19 @@
         tt[s] = jnp.broadcast_to(wanted[:R, s : s + 1], (R, 128))
     pl.semaphore_wait(barrier, len(peers))
 
-    sent_y = {d: send(qbuf.at[0, 0], qbuf.at[0, d], on_y(d)) for d in y_order}
-    sent_x = {}
-    sides = {1: [], 2: [1]}.get(X, [1, X - 1])
-    for e in sides:
-        sent_x[e, 0] = send(qbuf.at[0, 0], qbuf.at[e, 0], on_x(e))
-    sent_gain = send(gs.at[k], gs.at[k], on_pair(1))
-    sent_head = {j: send(wh.at[:, 0:128], wh.at[:, j * 128 : (j + 1) * 128], on_pair(j)) for j in (2, 1)}
-    for d in y_order:
-        recv(sent_y[d], qbuf.at[0, d])
-        for e in sides:
-            sent_x[e, d] = send(qbuf.at[0, d], qbuf.at[e, d], on_x(e))
-    for e in x_order[len(sides) :]:
-        for d in [0] + y_order:
-            sent_x[e, d] = send(qbuf.at[0, d], qbuf.at[e, d], on_x(e))
-    for copy in local[6:]:
-        copy.wait()
-    sent_proj = {d: send(wo.at[y], wo.at[y], on_y(d)) for d in y_order}
-    sent_resid = {e: send(rb.at[x], rb.at[x], on_x(e)) for e in x_order}
-
     scale = math.log2(math.e) / math.sqrt(HEAD_SIZE)
     group = Y * R
 
-    def attend(e, s):
-        logs = {}
+    def attend(members, s):
+        logs = [{} for _ in members]
         for h in range(heads):
             at = slice(h * HEAD_SIZE, (h + 1) * HEAD_SIZE)
-            block = qbuf[e, :, s, :, at].reshape(group, HEAD_SIZE)
+            block = [qbuf[s, e, :, :, at].reshape(group, HEAD_SIZE) for e in members]
             scores = lax.dot_general(
-                block, keys[s, :, at], (((1,), (1,)), ((), ())), preferred_element_type=F32
+                jnp.concatenate(block, axis=0),
+                keys[s, :, at],
+                (((1,), (1,)), ((), ())),
+                preferred_element_type=F32,
             )
             top = jnp.max(scores, -1, keepdims=True)
             weights = jnp.exp2((scores - top) * scale)
@@ -187,98 +178,185 @@
             summed = jnp.dot(
                 weights.astype(BF16), values[s, :, at], preferred_element_type=F32
             )
-            obuf[e, s, :, at] = (summed / total).astype(BF16)
-            logs[s * heads + h] = top * (1.0 / math.sqrt(HEAD_SIZE)) + jnp.log(total)
-        ostat[e, s] = columns_to_tile(logs)
-
-    for s in range(S):
-        attend(0, s)
+            summed = (summed / total).astype(BF16)
+            log_sum = top * (1.0 / math.sqrt(HEAD_SIZE)) + jnp.log(total)
+            for place, e in enumerate(members):
+                rows = slice(place * group, (place + 1) * group)
+                obuf[e, s, :, at] = summed[rows]
+                logs[place][h] = log_sum[rows]
+        for place, e in enumerate(members):
+            ostat[e, s] = columns_to_tile(logs[place])[:heads]
+
+    def attend_first():
+        attend([0], 0)
+
+    sides = {1: [], 2: [1]}.get(X, [1, X - 1])
+    opposite, y_steps = x_order[len(sides) :], [0] + y_order
+    sent_y, sent_x = {}, {}
+    for s in range(S):
+        for d in y_order:
+            sent_y[s, d] = send(qbuf.at[s, 0, 0], qbuf.at[s, 0, d], on_y(d))
+    sent_gain = send(gs.at[k], gs.at[k], on_pair(1))
+    sent_head = {j: send(wh.at[:, 0:128], wh.at[:, j * 128 : (j + 1) * 128], on_pair(j)) for j in (2, 1)}
+
+    def queries_on(s, ways, d):
+        for e in ways:
+            sent_x[s, e, d] = send(qbuf.at[s, 0, d], qbuf.at[s, e, d], on_x(e))
+
+    for s in range(S):
+        queries_on(s, sides, 0)
+        for at, d in enumerate(y_order):
+            recv(sent_y[s, d], qbuf.at[s, 0, d])
+            queries_on(s, sides, d)
+            if at >= 2:
+                queries_on(s, opposite, y_steps[at - 2])
+        for d in y_steps[max(Y - 3, 0) :]:
+            queries_on(s, opposite, d)
+        if s == 0:
+            for copy in local[5:]:
+                copy.wait()
+            attend_first()
+    y_direct = [d for d in y_order if Y < 8 or min(d, Y - d) <= 2]
+    sent_proj = {d: send(wo.at[k, y], wo.at[k, y], on_y(d)) for d in reversed(y_direct)}
+
+    def proj_from(d):
+        return wo.at[k, lax.rem(y - d + Y, Y)]
+
+    def half_of(ref, first):
+        return ref.at[: W // 2] if first else ref.at[W // 2 :]
+
+
+    def spread_x(numbers, block, slots, s):
+        @pl.when(k == s)
+        def _():
+            slots[x, k] = block[s]
+            for e in x_order:
+                copy_of(numbers["same", e], block.at[s], slots.at[x, k], on_x(e)).start()
+
+        @pl.when(k != s)
+        def _():
+            for e in [0] + x_order:
+                there = other_core(on_x(e))
+                copy_of(numbers["other", e], block.at[s], slots.at[x, k], there).start()
+
+    def numbers_for(block, slots):
+        numbers = {}
+        for way, steps in (("same", x_order), ("other", [0] + x_order)):
+            for e in steps:
+                numbers[way, e] = len(started)
+                started.append(copy_of(len(started), block.at[0], slots.at[x, k], on_pair(1)))
+        return numbers
+
+    def gathered_x(numbers, slots):
+        for (way, e), number in numbers.items():
+            recv(number, slots.at[lax.rem(x - e + X, X), k if way == "same" else 1 - k])
+
+    sent_resid = numbers_for(resid, rb)
+    for s in range(S):
+        spread_x(sent_resid, resid, rb, s)
+
+    sent_o, sent_s = {}, {}
+
+    def attend_others(members, s):
+        for e in members:
+            for d in y_steps:
+                recv(sent_x[s, e, d], qbuf.at[s, e, d])
+        if members:
+            attend(members, s)
+        for e in members:
+            sent_o[e, s] = send(obuf.at[e, s], xr.at[e, s], on_x(-e))
+            sent_s[e, s] = send(ostat.at[e, s], xs.at[e, s], on_x(-e))
+
+    attend_others(sides, 0)
+    attend_others(opposite, 0)
     recv(sent_gain, gs.at[1 - k])
     gb[z] = gs[...]
     sent_gains = {d: send(gs, gb.at[z], on_z(d)) for d in z_order}
-    sent_o, sent_s = {}, {}
-    units = [(e, s) for s in range(S) for e in sides]
-    for e, s in units + [(e, s) for e in x_order[len(sides) :] for s in range(S)]:
-        if s == 0:
-            for d in [0] + y_order:
-                recv(sent_x[e, d], qbuf.at[e, d])
-        attend(e, s)
-        sent_o[e, s] = send(obuf.at[e, s], xr.at[e, s], on_x(-e))
-        sent_s[e, s] = send(ostat.at[e, s], xs.at[e, s], on_x(-e))
-
-    sent_yo, sent_ys, log_sums = {}, {}, []
+    attend_others(sides, 1)
+    attend([0], 1)
+    attend_others(opposite, 1)
+
+    for d in y_direct:
+        recv(sent_proj[d], proj_from(d))
+    if Y == 8:
+        for step, d in ((1, 2), (-1, Y - 2)):
+            sent_proj[d + step] = send(proj_from(d), proj_from(d), on_y(step))
+        for step, d in ((2, 2), (-2, Y - 2)):
+            part = (step > 0, Y // 2)
+            sent_proj[part] = send(*[half_of(proj_from(d), step > 0)] * 2, on_y(step))
+
+    sent_yo, sent_ys = {}, {}
     for s in range(S):
         for e in x_order:
             recv(sent_o[e, s], xr.at[e, s])
             recv(sent_s[e, s], xs.at[e, s])
-        shares, log_sum = merge([ostat[0, s]] + [xs[e, s] for e in x_order])
-        log_sums.append(log_sum)
+        shares, ystat[s] = merge([ostat[0, s]] + [xs[e, s] for e in x_order])
         table = transposed(shares)
         for h in range(heads):
             at = slice(h * HEAD_SIZE, (h + 1) * HEAD_SIZE)
             total = None
             for place, e in enumerate([0] + x_order):
-                column = place * 8 + s * heads + h
+                column = place * heads + h
                 part = obuf[0, s, :, at] if e == 0 else xr[e, s, :, at]
                 part = part.astype(F32) * table[:group, column : column + 1]
                 total = part if total is None else total + part
             yb[s, :, :, at] = total.reshape(Y, R, HEAD_SIZE).astype(BF16)
         for d in y_order:
             sent_yo[d, s] = send(yb.at[s, d], yr.at[s, d], on_y(-d))
-    row = lax.broadcasted_iota(jnp.int32, (8, 128), 0)
-    ystat[...] = jnp.where(row < heads, log_sums[0], log_sums[1])
-    for d in y_order:
-        sent_ys[d] = send(ystat, ys.at[d], on_y(-d))
-    for d in y_order:
-        recv(sent_ys[d], ys.at[d])
-    shares, _ = merge([ystat[...]] + [pltpu.roll(ys[d], 128 - d * R, 1) for d in y_order])
-    table = transposed(shares)
+            sent_ys[d, s] = send(ystat.at[s], ys.at[s, d], on_y(-d))
+    if Y == 8:
+        for d in (3, Y - 3):
+            recv(sent_proj[d], proj_from(d))
+        for first in (True, False):
+            recv(sent_proj[first, Y // 2], half_of(proj_from(Y // 2), first))
+    sent_proj = send(wo.at[k], wo.at[k], on_pair(1))
+    sent_rows = numbers_for(ab, at_x)
     for s in range(S):
         for d in y_order:
             recv(sent_yo[d, s], yr.at[s, d])
+            recv(sent_ys[d, s], ys.at[s, d])
+        shares, _ = merge([ystat[s]] + [pltpu.roll(ys[s, d], 128 - d * R, 1) for d in y_order])
+        table = transposed(shares)
         for h in range(heads):
             at = slice(h * HEAD_SIZE, (h + 1) * HEAD_SIZE)
             total = None
             for place, d in enumerate([0] + y_order):
-                column = place * 8 + s * heads + h
+                column = place * heads + h
                 part = yb[s, 0, :, at] if d == 0 else yr[s, d, :, at]
                 part = part.astype(F32) * table[:R, column : column + 1]
                 total = part if total is None else total + part
-            ab[x, s, :, at] = total.astype(BF16)
-
-    sent = {e: send(ab.at[x], ab.at[x], on_x(e)) for e in x_order}
-    for d in y_order:
-        recv(sent_proj[d], wo.at[lax.rem(y - d + Y, Y)])
-    for e in x_order:
-        recv(sent_resid[e], rb.at[lax.rem(x - e + X, X)])
-    for e in x_order:
-        recv(sent[e], ab.at[lax.rem(x - e + X, X)])
-    rows = X * S * R
-    attended = ab[...].reshape(rows, W)
-    residual = rb[...].reshape(rows, W).astype(F32)
+            ab[s, :, at] = total.astype(BF16)
+        spread_x(sent_rows, ab, at_x, s)
+
+    recv(sent_proj, wo.at[1 - k])
+    gathered_x(sent_resid, rb)
+    gathered_x(sent_rows, at_x)
+    eight, half = R // 2, cols // 2
+    attended = jnp.concatenate([at_x[:, c].reshape(X * R, W) for c in range(2)], axis=1)
     width = wo.shape[-1]
     for j in range(cols // W):
-        if width < W:
-            each = W // width
-            weights = jnp.concatenate([wo[j * each + i] for i in range(each)], axis=1)
-        else:
-            first = j * W
-            weights = wo[first // width, :, first % width : first % width + W]
-        mine = (tp == x * (cols // W) + j).astype(F32)
-        part = jnp.dot(attended, weights, preferred_element_type=F32) + residual * mine
-        part = part.reshape(X * S, 2, R // 2, W)
-        for half in range(2):
-            pb[half, :, :, j * W : (j + 1) * W] = part[:, half]
-
-    eight, half = R // 2, cols // 2
-    sent_core = send(pb.at[1 - k], cb, on_pair(1))
-    recv(sent_core, cb)
-    summed = pb[k] + cb[...]
+        weights = []
+        for c in range(2):
+            if width < W:
+                each = W // width
+                weights.append(
+                    jnp.concatenate([wo[c, j * each + i] for i in range(each)], axis=1)
+                )
+            else:
+                first = j * W
+                weights.append(wo[c, first // width, :, first % width : first % width + W])
+        part = jnp.dot(attended, jnp.concatenate(weights, axis=0), preferred_element_type=F32)
+        block = x * (cols // W) + j
+        mine = (z == block // 2).astype(F32)
+        part = part + rb[:, j % 2].reshape(X * R, W).astype(F32) * mine
+        own[:, :, j * W : (j + 1) * W] = part.reshape(Z, eight, W)
+
+    summed = own[...]
     zs[...] = jnp.concatenate([summed[:, :, :half], summed[:, :, half:]], axis=1).astype(BF16)
     sent = {d: send(zs.at[lax.rem(z + d, Z)], zr.at[d], on_z(d)) for d in z_order}
     for d in z_order:
         recv(sent_gains[d], gb.at[lax.rem(z - d + Z, Z)])
-    stream = pb[k, z] + cb[z]
+    stream = own[z]
     for d in z_order:
         recv(sent[d], zr.at[d])
         both = zr[d].astype(F32)
@@ -293,8 +371,8 @@
     def piece(i, d, e):
         return ex.at[lax.rem(x - i + X, X), lax.rem(y - d + Y, Y), near(e)]
 
-    y_direct = [d for d in y_order if Y < 8 or min(d, Y - d) <= 2]
     z_steps = [0] + zh_order
+    x_first = z_steps[-1]
     under_way, busy = [], {}
 
     def launch(now, axis, step, i, d, e):
@@ -322,22 +400,23 @@
                 launch(now, "y", 2 * step, i, d, e)
 
     def arrived(now, i, d, e):
-        if e == 0 or i == 0:
-            spread_y(now, i, d, e)
-        if e and i == 0:
+        if e == x_first and i == d == 0:
+            for step in x_order:
+                launch(now, "x", step, i, d, e)
+        elif e != x_first and i == 0:
             for step in sides:
                 launch(now, "x", step, i, d, e)
-        elif e and X == 4 and i == (1 if (z_steps.index(e) + d) % 2 else X - 1):
+        if e == x_first or i == 0:
+            spread_y(now, i, d, e)
+        elif X == 4 and i == (1 if (z_steps.index(e) + d) % 2 else X - 1):
             launch(now, "x", 1 if i == 1 else -1, i, d, e)
 
     for e in zh_order:
         launch(0.0, "z", e, 0, 0, 0)
-    for i in x_order:
-        launch(0.0, "x", i, 0, 0, 0)
-    spread_y(0.0, 0, 0, 0)
+    arrived(0.0, 0, 0, 0)
     lane = lax.broadcasted_iota(jnp.int32, (eight, 128), 1)
     squares = jnp.sum(stream * stream, -1, keepdims=True)
-    wanted = tt[s_own, pl.ds(pl.multiple_of(k * eight, eight), eight), :] * (x == zh).astype(F32)
+    wanted = tt[k, pl.ds(pl.multiple_of(parity * eight, eight), eight), :] * (x == zh).astype(F32)
     ea[zh] = jnp.where(lane == 0, squares, jnp.where(lane == 1, wanted, 0.0))
     sent_az = {e: send(ea.at[zh], ea.at[zh], on_z(2 * e)) for e in zh_order}
     recv(sent_head[2], wh.at[:, 256:384])
@@ -428,24 +507,29 @@
             hit = (lane + first).astype(F32) == wanted
             picked = picked + jnp.where(hit, logits[:, j * 128 : (j + 1) * 128], 0.0)
         tile = columns_to_tile(
-            {i: top + jnp.log(sums), 4 + i: jnp.sum(picked, -1, keepdims=True)}
+            {i: top + jnp.log(sums), 2 + i: jnp.sum(picked, -1, keepdims=True)}
         )
         fin = tile if fin is None else fin + tile
-    ft[tp] = fin
+    ft[tp] = fin[:4]
+
+    row = lax.broadcasted_iota(jnp.int32, (8, 128), 0)
 
     def combine(parts):
         _, log_sum = merge(parts)
-        row = lax.broadcasted_iota(jnp.int32, (8, 128), 0)
-        return jnp.where(row < 4, log_sum, functools.reduce(jnp.add, parts))
+        logs = lax.broadcasted_iota(jnp.int32, parts[0].shape, 0) < parts[0].shape[0] // 2
+        return jnp.where(logs, log_sum, functools.reduce(jnp.add, parts))
 
     sent = {d: send(ft.at[tp], ft.at[tp], on_tp(d)) for d in range(1, 2 * Z)}
+    settled = len(started)
+    for copy in started:
+        copy.wait_send()
     for d in range(1, 2 * Z):
         recv(sent[d], ft.at[lax.rem(tp - d + 2 * Z, 2 * Z)])
     for s in range(S):
         first, second = (
-            combine([ft[4 * i + 2 * s + core] for i in range(ZH)]) for core in range(2)
+            combine([ft[4 * i + 2 * upper + s] for i in range(ZH)]) for upper in range(2)
         )
-        fy[y, s] = jnp.where(lax.rem(row, 4) < 2, first, pltpu.roll(second, 2, 0))
+        fy[y, s] = jnp.concatenate([first[:2], second[:2], first[2:], second[2:]], axis=0)
     sent = {d: send(fy.at[y], fy.at[y], on_y(d)) for d in y_order}
     for d in y_order:
         recv(sent[d], fy.at[lax.rem(y - d + Y, Y)])
@@ -460,7 +544,7 @@
     from_x = lax.rem(lane, block) // eight
     slot = (from_x * Y + from_y) * R + (row // 2) * eight + lax.rem(lane, eight)
     counted = (row < 4) & (from_y < Y)
-    sample_sum, own = None, []
+    sample_sum, tokens = None, []
     first = lax.rem(y, per_tile) * block + x * eight
     member = lax.broadcasted_iota(jnp.int32, (R, 128), 0)
     place = lax.broadcasted_iota(jnp.int32, (R, 128), 1) == first + lax.rem(member, eight)
@@ -474,19 +558,19 @@
         in_first = y < per_tile
         lower = jnp.where(in_first, tile[0:1], tile[1:2])
         upper = jnp.where(in_first, tile[2:3], tile[3:4])
-        own.append(jnp.where(place, jnp.where(member < eight, lower, upper), 0.0))
+        tokens.append(jnp.where(place, jnp.where(member < eight, lower, upper), 0.0))
     loss[...] = sample_sum * (1.0 / S)
-    token = jnp.sum(transposed(own), 0, keepdims=True)
-    for s in range(S):
-        out[s : s + 1, :] = token[:, s * R : (s + 1) * R]
-    for copy in started:
+    token = jnp.sum(transposed(tokens), 0, keepdims=True)
+    for s in range(S):
+        out[0, s : s + 1, :] = token[:, s * R : (s + 1) * R]
+    for copy in started[settled:]:
         copy.wait_send()
     assert len(started) == copies(X, Y, Z), len(started)
 
 
 def copies(X, Y, Z):
     x, y, z, zh = X - 1, Y - 1, Z - 1, Z // 2 - 1
-    count = y + x + 1 + 2 + x * y + y + x + z + 4 * x + 3 * y + x + 1 + z
+    count = 2 * (y + x + x * y) + 3 + (8 if Y == 8 else y) + 2 * (2 * x + 1) + z + 4 * x + 4 * y + 1 + z
     count += X * Y * Z // 2 - 1 + 1 + zh + y + x
     return count + 2 * Z - 1 + y + x
 
@@ -513,34 +597,32 @@
     ZH = Z // 2
     block = ZH * (R // 2)
     tiles = -(-Y * block // 128)
-    frequency = ROPE_BASE ** (-2.0 * jnp.arange(HEAD_SIZE // 2, dtype=F32) / HEAD_SIZE)
-    frequency = jnp.concatenate([frequency, frequency])[None]
     vmem = pl.BlockSpec(memory_space=pltpu.VMEM)
     hbm = pl.BlockSpec(memory_space=pl.ANY)
     scratch = [
         ((S, R, W), BF16),
         ((S, R), jnp.int32),
-        ((1, HEAD_SIZE), F32),
         ((S, R), jnp.int32),
+        ((S, R, W), BF16),
         ((W,), BF16),
         ((S, L, W), BF16),
         ((S, L, W), BF16),
-        ((X, Y, S, R, W), BF16),
+        ((S, X, Y, R, W), BF16),
         ((X, S, Y * R, W), BF16),
-        ((X, S, 8, 128), F32),
+        ((X, S, W // HEAD_SIZE, 128), F32),
         ((X, S, Y * R, W), BF16),
-        ((X, S, 8, 128), F32),
+        ((X, S, W // HEAD_SIZE, 128), F32),
         ((S, Y, R, W), BF16),
-        ((8, 128), F32),
+        ((S, W // HEAD_SIZE, 128), F32),
         ((S, Y, R, W), BF16),
-        ((Y, 8, 128), F32),
-        ((X, S, R, W), BF16),
-        ((X, S, R, W), BF16),
+        ((S, Y, W // HEAD_SIZE, 128), F32),
+        ((S, R, W), BF16),
+        ((X, 2, R, W), BF16),
+        ((X, 2, R, W), BF16),
         ((2, 8, W), F32),
         ((Z, 2, 8, W), F32),
-        ((Y, W, out_proj.shape[1]), BF16),
+        ((2, Y, W, out_proj.shape[1]), BF16),
         ((D, 4 * 128), BF16),
-        ((2, Z, R // 2, cols), F32),
         ((Z, R // 2, cols), F32),
         ((S, R, 128), F32),
         ((Z, R, cols // 2), BF16),
@@ -550,20 +632,20 @@
         ((Y, 8, 128), F32),
         ((X, tiles, 8, 128), F32),
         ((Y * block, 4 * 128), F32),
-        ((2 * Z, 8, 128), F32),
+        ((2 * Z, 4, 128), F32),
         ((Y, S, 8, 128), F32),
         ((X, S, 8, 128), F32),
     ]
     count = copies(X, Y, Z)
-    smem = pl.BlockSpec(memory_space=pltpu.SMEM)
     token_nll, loss = pl.pallas_call(
         functools.partial(kernel, sizes),
-        out_shape=[jax.ShapeDtypeStruct((S, R), F32), jax.ShapeDtypeStruct((1, 1), F32)],
-        in_specs=[smem] * 2 + [hbm] * 10,
+        out_shape=[jax.ShapeDtypeStruct((1, S, R), F32), jax.ShapeDtypeStruct((1, 1), F32)],
+        in_specs=[hbm] * 11,
         out_specs=[vmem, vmem],
-        scratch_shapes=[pltpu.VMEM(*shape) for shape in scratch]
+        scratch_shapes=[pltpu.SMEM((S,), jnp.int32)] * 2
+        + [pltpu.VMEM(*shape) for shape in scratch]
         + [
-            pltpu.SemaphoreType.DMA((10,)),
+            pltpu.SemaphoreType.DMA((11,)),
             pltpu.SemaphoreType.DMA((count,)),
             pltpu.SemaphoreType.DMA((count,)),
         ],
@@ -572,10 +654,10 @@
         ),
         name="cloze",
     )(
-        live_rows, mask_total, queries, positions, frequency, targets, residual_rows,
+        live_rows, mask_total, queries, positions, targets, residual_rows,
         norm_gain, cached_keys, cached_values, out_proj, head_weight,
     )
-    return (token_nll, loss.reshape(()))
+    return (token_nll.reshape(S, R), loss.reshape(()))
 
 
 def solution(mesh):

time: 102 us -> 96.3 us (0.944)
  Pallas kernels: 97.6 us -> 92.4 us
    pallas_call x1, Pallas kernels: 97.6 us -> 92.4 us  [on_device(): pl.pallas_call(functools.partial(kernel, sizes), out_shape=[jax.ShapeDtyp...]
where the time goes in v3:
time: 96.3 us; the launch traced here: 96 us
  Pallas kernels  92.4 us (96%)
  between operations  2.41 us (3%)
  local copies, waits for them, and re-layouts  1.21 us (1%)
    pallas_call x1, Pallas kernels, on_device(): pl.pallas_call(functools.partial(kernel, sizes), out_shape=[jax.ShapeDtyp...  92.4 us

profile of v3, /device:TPU:1, one launch (start us, length us, event | category | flops | bytes accessed | tf_op | source)
XLA Modules:
  0.0 96.0 jit_solution(12715101883117172792)
XLA Ops:
  0.6 92.4 %cloze.1 = (f32[1,2,16]{2,1,0:T(2,128)}, f32[1,1]{1,0:T(1,128)}) custom-call(s32[2]{0:T(128)} %live_hbm.1, s32[2]{0:T(128)} %mask_hbm.1, bf16[2,16,256]{2,1,0:T(8,128)(2,1)} %q_hbm.1, s32[2,16]{1,0:T(2,128)} %positions_hbm.1, s32[2,16]{1,0:T(2,128)} %targets_hbm.1, bf16[2,16,256]{2,1,0:T(8,128)(2,1)} %resid_hbm.1, bf16[256]{0:T(256)(128)(2,1)} %gain_hbm.1, ...), custom_call_target="tpu_custom_call" | custom-call | tf_op jit(solution)/shard_map/cloze/pallas_call | solution.py:640
  93.1 0.0 copy-start
  93.1 0.6 copy-done
  93.7 0.6 copy.15
Async XLA Ops:
  93.1 0.7 copy-start

commit v4 on v3

--- a/solution.py
+++ b/solution.py
@@ -51,9 +51,9 @@
     sizes,
     live_hbm, mask_hbm, q_hbm, positions_hbm, targets_hbm, resid_hbm, gain_hbm,
     keys_hbm, values_hbm, proj_hbm, head_hbm,
-    out, loss,
+    out_hbm, loss_hbm,
     live_rows, mask_total, q, positions, targets, resid, gain, keys, values, qbuf, obuf, ostat,
-    xr, xs, yb, ystat, yr, ys, ab, at_x, rb, gs, gb, wo, wh, own, tt, zs, zr, ea, ex, ya, xa, lg, ft, fy, fx,
+    xr, xs, yb, ystat, yr, ys, ab, at_x, rb, gb, wo, wh, own, tt, zs, zr, ea, ex, ya, xa, lg, ft, fy, fx, out, loss,
     local_sem, send_sem, recv_sem,
 ):
     X, Y, Z = sizes
@@ -152,7 +152,7 @@
             qbuf[s, 0, 0, :, at] = turned.astype(BF16)
     for copy in local[2:5]:
         copy.wait()
-    gs[k] = jnp.broadcast_to(gain[...].astype(F32).reshape(1, W), (8, W))
+    gb[tp] = gain[...].astype(F32).reshape(1, W)
     wanted = column_table(targets)
     for s in range(S):
         tt[s] = jnp.broadcast_to(wanted[:R, s : s + 1], (R, 128))
@@ -196,7 +196,7 @@
     for s in range(S):
         for d in y_order:
             sent_y[s, d] = send(qbuf.at[s, 0, 0], qbuf.at[s, 0, d], on_y(d))
-    sent_gain = send(gs.at[k], gs.at[k], on_pair(1))
+    sent_gains = {d: send(gb.at[tp], gb.at[tp], on_tp(d)) for d in range(1, 2 * Z)}
     sent_head = {j: send(wh.at[:, 0:128], wh.at[:, j * 128 : (j + 1) * 128], on_pair(j)) for j in (2, 1)}
 
     def queries_on(s, ways, d):
@@ -267,14 +267,10 @@
             sent_o[e, s] = send(obuf.at[e, s], xr.at[e, s], on_x(-e))
             sent_s[e, s] = send(ostat.at[e, s], xs.at[e, s], on_x(-e))
 
-    attend_others(sides, 0)
-    attend_others(opposite, 0)
-    recv(sent_gain, gs.at[1 - k])
-    gb[z] = gs[...]
-    sent_gains = {d: send(gs, gb.at[z], on_z(d)) for d in z_order}
-    attend_others(sides, 1)
     attend([0], 1)
-    attend_others(opposite, 1)
+    for s in range(S):
+        attend_others(sides, s)
+        attend_others(opposite, s)
 
     for d in y_direct:
         recv(sent_proj[d], proj_from(d))
@@ -354,14 +350,14 @@
     summed = own[...]
     zs[...] = jnp.concatenate([summed[:, :, :half], summed[:, :, half:]], axis=1).astype(BF16)
     sent = {d: send(zs.at[lax.rem(z + d, Z)], zr.at[d], on_z(d)) for d in z_order}
-    for d in z_order:
-        recv(sent_gains[d], gb.at[lax.rem(z - d + Z, Z)])
+    for d in range(1, 2 * Z):
+        recv(sent_gains[d], gb.at[lax.rem(tp - d + 2 * Z, 2 * Z)])
     stream = own[z]
     for d in z_order:
         recv(sent[d], zr.at[d])
         both = zr[d].astype(F32)
         stream = stream + jnp.concatenate([both[:eight], both[eight:]], axis=1)
-    gains = [gb[x * (cols // W // 2) + j // 2, j % 2] for j in range(cols // W)]
+    gains = [gb[x * (cols // W) + j] for j in range(cols // W)]
     scaled = stream * jnp.concatenate(gains, axis=1)
     ex[x, y, zh] = jnp.concatenate([scaled[:, :half], scaled[:, half:]], axis=0).astype(BF16)
 
@@ -450,28 +446,27 @@
 
     slots = Y * ZH * eight
 
-    def multiply(i):
+    def multiply(i, e):
         if not complete:
             for j in (1, 3):
                 recv(sent_head[j], wh.at[:, j * 128 : (j + 1) * 128])
-        from_x = lax.rem(x - i + X, X)
-        block = ex[from_x].reshape(Y * ZH * R, half)
+        from_x, from_z = lax.rem(x - i + X, X), near(e)
+        block = ex[from_x, :, from_z].reshape(Y * R, half)
         total = None
         for upper in range(2):
             start = pl.multiple_of(from_x * cols + upper * half, half)
             part = jnp.dot(block, wh[pl.ds(start, half), :], preferred_element_type=F32)
-            part = part.reshape(Y * ZH, 2, eight, 4 * 128)[:, upper]
+            part = part.reshape(Y, 2, eight, 4 * 128)[:, upper]
             total = part if total is None else total + part
-        total = total.reshape(slots, 4 * 128)
-        if complete:
-            lg[...] += total
+        if e in complete:
+            lg[:, from_z] += total
         else:
-            lg[...] = total
-        complete.append(i)
+            lg[:, from_z] = total
+        complete.append(e)
 
     complete = []
-    missing = {i: Y * ZH for i in range(X)}
-    missing[0] -= 1
+    missing = {(i, e): Y for i in range(X) for e in z_steps}
+    missing[0, 0] -= 1
     later = [(6.0, rows_along_y), (11.0, rows_along_x)]
     while under_way:
         now, number, place = heapq.heappop(under_way)
@@ -479,14 +474,14 @@
             later.pop(0)[1]()
         recv(number, piece(*place))
         arrived(now, *place)
-        missing[place[0]] -= 1
-        if missing[place[0]] == 0 and under_way:
-            multiply(place[0])
+        i, _, e = place
+        missing[i, e] -= 1
+        if missing[i, e] == 0:
+            multiply(i, e)
     for _, step in later:
         step()
-    for i in range(X):
-        if i not in complete:
-            multiply(i)
+    if Y == 1:
+        multiply(0, 0)
     for e in x_order:
         recv(sent_ax[e], xa.at[lax.rem(x - e + X, X)])
     span = min(128, slots)
@@ -496,7 +491,7 @@
         for from_x in range(1, X):
             total = total + xa[from_x, i]
         table = transposed([lax.rsqrt(total * (1.0 / (X * cols)) + NORM_EPSILON), total])
-        logits = lg[i * span : (i + 1) * span, :] * table[:span, 0:1]
+        logits = lg[i * per_tile : (i + 1) * per_tile].reshape(span, 4 * 128) * table[:span, 0:1]
         wanted = table[:span, 9:10]
         top = jnp.max(logits, -1, keepdims=True)
         sums = jnp.sum(jnp.exp(logits - top), -1, keepdims=True)
@@ -563,14 +558,22 @@
     token = jnp.sum(transposed(tokens), 0, keepdims=True)
     for s in range(S):
         out[0, s : s + 1, :] = token[:, s * R : (s + 1) * R]
+    finished = [
+        pltpu.make_async_copy(out, out_hbm, local_sem.at[0]),
+        pltpu.make_async_copy(loss, loss_hbm, local_sem.at[1]),
+    ]
+    for copy in finished:
+        copy.start()
     for copy in started[settled:]:
         copy.wait_send()
+    for copy in finished:
+        copy.wait()
     assert len(started) == copies(X, Y, Z), len(started)
 
 
 def copies(X, Y, Z):
     x, y, z, zh = X - 1, Y - 1, Z - 1, Z // 2 - 1
-    count = 2 * (y + x + x * y) + 3 + (8 if Y == 8 else y) + 2 * (2 * x + 1) + z + 4 * x + 4 * y + 1 + z
+    count = 2 * (y + x + x * y) + 2 + 2 * Z - 1 + (8 if Y == 8 else y) + 2 * (2 * x + 1) + 4 * x + 4 * y + 1 + z
     count += X * Y * Z // 2 - 1 + 1 + zh + y + x
     return count + 2 * Z - 1 + y + x
 
@@ -597,7 +600,6 @@
     ZH = Z // 2
     block = ZH * (R // 2)
     tiles = -(-Y * block // 128)
-    vmem = pl.BlockSpec(memory_space=pltpu.VMEM)
     hbm = pl.BlockSpec(memory_space=pl.ANY)
     scratch = [
         ((S, R, W), BF16),
@@ -619,8 +621,7 @@
         ((S, R, W), BF16),
         ((X, 2, R, W), BF16),
         ((X, 2, R, W), BF16),
-        ((2, 8, W), F32),
-        ((Z, 2, 8, W), F32),
+        ((2 * Z, 1, W), F32),
         ((2, Y, W, out_proj.shape[1]), BF16),
         ((D, 4 * 128), BF16),
         ((Z, R // 2, cols), F32),
@@ -631,17 +632,19 @@
         ((X, Y, ZH, R, cols // 2), BF16),
         ((Y, 8, 128), F32),
         ((X, tiles, 8, 128), F32),
-        ((Y * block, 4 * 128), F32),
+        ((Y, ZH, R // 2, 4 * 128), F32),
         ((2 * Z, 4, 128), F32),
         ((Y, S, 8, 128), F32),
         ((X, S, 8, 128), F32),
+        ((1, S, R), F32),
+        ((1, 1), F32),
     ]
     count = copies(X, Y, Z)
     token_nll, loss = pl.pallas_call(
         functools.partial(kernel, sizes),
         out_shape=[jax.ShapeDtypeStruct((1, S, R), F32), jax.ShapeDtypeStruct((1, 1), F32)],
         in_specs=[hbm] * 11,
-        out_specs=[vmem, vmem],
+        out_specs=[hbm, hbm],
         scratch_shapes=[pltpu.SMEM((S,), jnp.int32)] * 2
         + [pltpu.VMEM(*shape) for shape in scratch]
         + [

time: 96.3 us -> 95.3 us (0.990)
  Pallas kernels: 92.4 us -> 91.4 us
    pallas_call x1, Pallas kernels: 92.4 us -> 91.4 us  [on_device(): pl.pallas_call(functools.partial(kernel, sizes), out_shape=[jax.ShapeDtyp...]
where the time goes in v4:
time: 95.3 us; the launch traced here: 95 us
  Pallas kernels  91.4 us (96%)
  between operations  2.41 us (3%)
  local copies, waits for them, and re-layouts  1.21 us (1%)
    pallas_call x1, Pallas kernels, on_device(): pl.pallas_call(functools.partial(kernel, sizes), out_shape=[jax.ShapeDtyp...  91.4 us

profile of v4, /device:TPU:1, one launch (start us, length us, event | category | flops | bytes accessed | tf_op | source)
XLA Modules:
  0.0 95.0 jit_solution(3191189658655889888)
XLA Ops:
  0.6 91.4 %cloze.1 = (f32[1,2,16]{2,1,0:T(2,128)}, f32[1,1]{1,0:T(1,128)}) custom-call(s32[2]{0:T(128)} %live_hbm.1, s32[2]{0:T(128)} %mask_hbm.1, bf16[2,16,256]{2,1,0:T(8,128)(2,1)} %q_hbm.1, s32[2,16]{1,0:T(2,128)} %positions_hbm.1, s32[2,16]{1,0:T(2,128)} %targets_hbm.1, bf16[2,16,256]{2,1,0:T(8,128)(2,1)} %resid_hbm.1, bf16[256]{0:T(256)(128)(2,1)} %gain_hbm.1, ...), custom_call_target="tpu_custom_call" | custom-call | tf_op jit(solution)/shard_map/cloze/pallas_call | solution.py:643
  92.0 0.0 copy-start
  92.0 0.6 copy-done
  92.7 0.6 copy.15
Async XLA Ops:
  92.0 0.7 copy-start

commit v5 on v4

--- a/solution.py
+++ b/solution.py
@@ -371,6 +371,21 @@
     x_first = z_steps[-1]
     under_way, busy = [], {}
 
+    opposite_numbers = {}
+
+    def launch_opposite(core, now, step, i, d, e):
+        if (d, e) not in opposite_numbers:
+            opposite_numbers[d, e] = len(started)
+            started.append(copy_of(len(started), piece(i, d, e), piece(i, d, e), on_x(step)))
+
+        @pl.when(k == core)
+        def _():
+            copy_of(opposite_numbers[d, e], piece(i, d, e), piece(i, d, e), on_x(step)).start()
+
+        if core == 1:
+            number = opposite_numbers[d, e]
+            heapq.heappush(under_way, (now + 2.5, number, (2, d, e)))
+
     def launch(now, axis, step, i, d, e):
         size = {"x": X, "y": Y, "z": ZH}[axis]
         device = {"x": on_x, "y": on_y, "z": lambda n: on_z(2 * n)}[axis](step)
@@ -402,10 +417,15 @@
         elif e != x_first and i == 0:
             for step in sides:
                 launch(now, "x", step, i, d, e)
+            if X == 4 and Y == 8 and d not in [0] + y_direct:
+                launch_opposite(0, now, 2, i, d, e)
         if e == x_first or i == 0:
             spread_y(now, i, d, e)
         elif X == 4 and i == (1 if (z_steps.index(e) + d) % 2 else X - 1):
-            launch(now, "x", 1 if i == 1 else -1, i, d, e)
+            if d in [0] + y_direct:
+                launch(now, "x", 1 if i == 1 else -1, i, d, e)
+            else:
+                launch_opposite(1, now, 1 if i == 1 else -1, i, d, e)
 
     for e in zh_order:
         launch(0.0, "z", e, 0, 0, 0)

time: 95.3 us -> 93.8 us (0.984)
  Pallas kernels: 91.4 us -> 89.9 us
    pallas_call x1, Pallas kernels: 91.4 us -> 89.9 us  [on_device(): pl.pallas_call(functools.partial(kernel, sizes), out_shape=[jax.ShapeDtyp...]
where the time goes in v5:
time: 93.8 us; the launch traced here: 93.5 us
  Pallas kernels  89.9 us (96%)
  between operations  2.41 us (3%)
  local copies, waits for them, and re-layouts  1.21 us (1%)
    pallas_call x1, Pallas kernels, on_device(): pl.pallas_call(functools.partial(kernel, sizes), out_shape=[jax.ShapeDtyp...  89.9 us

profile of v5, /device:TPU:1, one launch (start us, length us, event | category | flops | bytes accessed | tf_op | source)
XLA Modules:
  0.0 93.5 jit_solution(13610964333180877045)
XLA Ops:
  0.6 89.9 %cloze.1 = (f32[1,2,16]{2,1,0:T(2,128)}, f32[1,1]{1,0:T(1,128)}) custom-call(s32[2]{0:T(128)} %live_hbm.1, s32[2]{0:T(128)} %mask_hbm.1, bf16[2,16,256]{2,1,0:T(8,128)(2,1)} %q_hbm.1, s32[2,16]{1,0:T(2,128)} %positions_hbm.1, s32[2,16]{1,0:T(2,128)} %targets_hbm.1, bf16[2,16,256]{2,1,0:T(8,128)(2,1)} %resid_hbm.1, bf16[256]{0:T(256)(128)(2,1)} %gain_hbm.1, ...), custom_call_target="tpu_custom_call" | custom-call | tf_op jit(solution)/shard_map/cloze/pallas_call | solution.py:663
  90.5 0.0 copy-start
  90.5 0.6 copy-done
  91.2 0.6 copy.15
Async XLA Ops:
  90.5 0.7 copy-start

commit v6 on v5

--- a/solution.py
+++ b/solution.py
@@ -393,12 +393,12 @@
         way = step % size
         way = way if 2 * way <= size else way - size
         link = (axis, way > 0)
-        busy[link] = max(now, busy.get(link, 0.0)) + 0.35 * abs(way)
+        busy[link] = max(now, busy.get(link, 0.0)) + 0.42 * abs(way)
         there = [i, d, e]
         at = "xyz".index(axis)
         there[at] = (there[at] + step) % size
         hops = abs(way) * (2 if axis == "z" else 1)
-        heapq.heappush(under_way, (busy[link] + 1.4 + 0.7 * hops, number, tuple(there)))
+        heapq.heappush(under_way, (busy[link] + 2.0 + 0.7 * hops, number, tuple(there)))
 
     def spread_y(now, i, d, e):
         if d == 0:

time: 93.8 us -> 93.6 us (level)
  no operation moved by 1% of the time
where the time goes in v6:
time: 93.6 us; the launch traced here: 93.1 us
  Pallas kernels  89.5 us (96%)
  between operations  2.41 us (3%)
  local copies, waits for them, and re-layouts  1.21 us (1%)
    pallas_call x1, Pallas kernels, on_device(): pl.pallas_call(functools.partial(kernel, sizes), out_shape=[jax.ShapeDtyp...  89.5 us

profile of v6, /device:TPU:1, one launch (start us, length us, event | category | flops | bytes accessed | tf_op | source)
XLA Modules:
  0.0 93.1 jit_solution(2048355496223924060)
XLA Ops:
  0.6 89.5 %cloze.1 = (f32[1,2,16]{2,1,0:T(2,128)}, f32[1,1]{1,0:T(1,128)}) custom-call(s32[2]{0:T(128)} %live_hbm.1, s32[2]{0:T(128)} %mask_hbm.1, bf16[2,16,256]{2,1,0:T(8,128)(2,1)} %q_hbm.1, s32[2,16]{1,0:T(2,128)} %positions_hbm.1, s32[2,16]{1,0:T(2,128)} %targets_hbm.1, bf16[2,16,256]{2,1,0:T(8,128)(2,1)} %resid_hbm.1, bf16[256]{0:T(256)(128)(2,1)} %gain_hbm.1, ...), custom_call_target="tpu_custom_call" | custom-call | tf_op jit(solution)/shard_map/cloze/pallas_call | solution.py:663
  90.2 0.0 copy-start
  90.2 0.6 copy-done
  90.8 0.6 copy.15
Async XLA Ops:
  90.2 0.7 copy-start
